TPU v7x, 256 devices: a whole 4x4x8 slice. The times are simulated.
256 devices in a mesh: row: 8 (over x, core), col: 8 (over z_lo, y), fiber: 4 (over z_hi).
Axes of the slice: x: 4, y: 4, z: 8 (z_hi: 4, z_lo: 2; z = z_hi * 2 + z_lo), core: 2. Of those that a mesh axis runs over, the one named last changes fastest.
Arguments:
- a_tiles: bfloat16 [64, 192, 128, 128], P('row', ('col', 'fiber'))
- a_cols: int32 [64, 192], P('row', ('col', 'fiber')), may hold values from 0 to 2047, as said below
- a_count: int32 [64, 32], P('row', ('col', 'fiber')), may hold values from 1 to 6, as said below
- b_tiles: bfloat16 [2048, 8, 128, 128], P(('row', 'fiber'), 'col'), may hold values from 0 to 1
- b_cols: int32 [2048, 8], P(('row', 'fiber'), 'col'), may hold values from 0 to 127, as said below
Outputs:
- normalized: float32 [64, 128, 128, 128], P(('row', 'fiber'), 'col')
Inputs may be any that keep to these rules, and one draw needn't show every extreme that they name: `a_cols`: a slot in part p of dimension 1 (p = s // 6) holds an inner tile index k with (k // 64) % 4 == p % 4. `a_count`: slots at or beyond the count hold no part of the matrix; some tile row has all slots live in every part. b_cols[k, c] lies in column block c, from c * 16 to (c + 1) * 16 - 1.
All inputs are finite; a program needn't handle non-finite values.
Results may differ from a plain program's by a relative error of at most 0.0003.
Values may be sent and summed in bfloat16 or wider, within the bound.
A program may use at most 128 MiB of HBM per device.

v0:
```python
import jax
import jax.numpy as jnp
from jax import lax
from jax.sharding import PartitionSpec as P

PT = 128
ASLOTS = 6


epsilon = 1e-06


def slot_mask(slot_counts, slot_total):
    position = jnp.arange(slot_total) % ASLOTS
    return position[None, :] < jnp.repeat(slot_counts, ASLOTS, axis=1)


def layer_position(tile_cols, block_rows, fibers):
    return tile_cols // (block_rows * fibers) * block_rows + tile_cols % block_rows


def grouped(values):
    rows = values.shape[0]
    groups = values.shape[1] // ASLOTS
    shaped = values.reshape((rows, groups, ASLOTS) + values.shape[2:])
    return jnp.swapaxes(shaped, 0, 1)


def add_products(totals, tile_set, partner, target, live):
    row_ids = jnp.arange(totals.shape[0])

    def one_group(carry, pieces):
        group_tiles, group_partner, group_target, group_live = pieces
        products = jnp.einsum(
            "msab,msbc->msac", group_tiles, group_partner, preferred_element_type=jnp.float32
        )
        products = jnp.where(group_live[:, :, None, None], products, 0.0)
        return (carry.at[row_ids[:, None], group_target].add(products), None)

    result, unused = lax.scan(
        one_group, totals, (grouped(tile_set), grouped(partner), grouped(target), grouped(live))
    )
    return result


def on_device(a_tiles, a_cols, a_count, b_tiles, b_cols):
    row_tiles = a_tiles.shape[0]
    tile_edge = a_tiles.shape[2]
    block_rows = b_tiles.shape[0]
    fibers = lax.axis_size("fiber")
    block_cols = PT // lax.axis_size("col")
    col_offset = lax.axis_index("col") * block_cols
    zero_tiles = jnp.zeros((row_tiles, block_cols, tile_edge, tile_edge), jnp.float32)
    panel_tiles, panel_cols = (
        lax.all_gather(b_tiles, "row", axis=0, tiled=True),
        lax.all_gather(b_cols, "row", axis=0, tiled=True),
    )
    tile_set = lax.all_gather(a_tiles, "col", axis=1, tiled=True)
    tile_cols = lax.all_gather(a_cols, "col", axis=1, tiled=True)
    slot_counts = lax.all_gather(a_count, "col", axis=1, tiled=True)
    slot_live = slot_mask(slot_counts, tile_set.shape[1])
    position = layer_position(tile_cols, block_rows, fibers)
    partner = panel_tiles[position, 0]
    target = panel_cols[position, 0] - col_offset
    partial_value = add_products(zero_tiles, tile_set, partner, target, slot_live)
    total_rows = row_tiles * lax.axis_size("row") * tile_edge
    own_rows = lax.psum_scatter(partial_value, "fiber", scatter_dimension=0, tiled=True)
    inflated = own_rows * own_rows
    column_total = lax.psum(jnp.sum(inflated, axis=(0, 2)), ("row", "fiber"))
    return inflated * (total_rows / (column_total + epsilon))[None, :, None, :]


def solution(mesh):
    placed = (
        P("row", ("col", "fiber"), None, None),
        P("row", ("col", "fiber")),
        P("row", ("col", "fiber")),
        P(("row", "fiber"), "col", None, None),
        P(("row", "fiber"), "col"),
    )
    return jax.shard_map(
        on_device,
        mesh=mesh,
        in_specs=placed,
        out_specs=P(("row", "fiber"), "col", None, None),
        check_vma=False,
    )
```

profile of v0, /device:TPU:1, one launch (start us, length us, event | category | flops | bytes accessed | tf_op | source)
XLA Modules:
  0.0 573.9 jit_solution(2784582012684004147)
XLA Ops:
  8.2 23.5 %all-gather = s32[8,6,8]{2,1,0:T(8,128)S(1)} all-gather(s32[1,6,8]{2,1,0:T(8,128)S(1)} %bitcast.74), channel_id=1, replica_groups=mesh['row'=8,'col'=8,'fiber'=4] {'col'}, dimensions={0}, use_global_device_ids=true | all-gather | bytes 1728 | tf_op jit(solution)/shard_map/all_gather | solution.py:59
  33.2 14.6 %all-reduce.1 = s32[512]{0:T(512)S(1)} all-reduce(s32[512]{0:T(512)S(1)} %bitcast_dynamic-update-slice_fusion), channel_id=1, replica_groups=mesh['row'=8,'col'=8,'fiber'=4] {'row'}, use_global_device_ids=true, to_apply=%add.1 | all-reduce | flops 512 | bytes 4096
  47.8 2.7 gather_fusion
  50.7 14.9 %all-gather.1 = s32[8,1,8]{2,1,0:T(1,128)S(1)} all-gather(s32[1,1,8]{2,1,0:T(1,128)S(1)} %bitcast.76), channel_id=1, replica_groups=mesh['row'=8,'col'=8,'fiber'=4] {'col'}, dimensions={0}, use_global_device_ids=true | all-gather | bytes 288 | tf_op jit(solution)/shard_map/all_gather | solution.py:60
  65.7 35.4 %all-gather.7.cloned.1.call-done = bf16[512,1,128,128]{3,2,1,0:T(8,128)(2,1)} async-done(((bf16[64,1,128,128]{3,2,1,0:T(8,128)(2,1)}), bf16[512,1,128,128]{3,2,1,0:T(8,128)(2,1)}) %all-gather.7.cloned.1.call-update) | async-done | bytes 16777232 | tf_op jit(solution)/shard_map/all_gather | solution.py:55
  101.1 20.6 %gather_fusion.1 = bf16[384,128,128]{2,1,0:T(8,128)(2,1)} fusion(bf16[512,1,128,128]{3,2,1,0:T(8,128)(2,1)} %all-gather.7.cloned.1.call-done, s32[384]{0:T(512)S(1)} %reshape.70), kind=kCustom, calls=%fused_computation.1 | custom fusion | bytes 25168896 | tf_op jit(solution)/shard_map/gather | solution.py:63
  121.6 115.4 %all-gather.5.cloned.1.call-done = bf16[8,48,128,128]{3,2,1,0:T(8,128)(2,1)} async-done(((bf16[8,6,128,128]{3,2,1,0:T(8,128)(2,1)}), bf16[8,48,128,128]{3,2,1,0:T(8,128)(2,1)}) %all-gather.5.cloned.1.call-update) | async-done | bytes 12582928 | tf_op jit(solution)/shard_map/all_gather | solution.py:58
  237.0 4.3 broadcast_in_dim.36
  241.3 96.1 %while.11 = (s32[]{:T(128)}, f32[8,16,128,128]{3,2,1,0:T(8,128)}, s32[8,8,6]{1,0,2:T(8,128)S(1)}, pred[8,8,6]{2,1,0:T(8,128)(4,1)S(1)}, bf16[8,8,6,128,128]{4,3,...) while((s32[]{:T(128)}, f32[8,16,128,128]{3,2,1,0:T(8,128)}, ...), condition=%wide.region_2.3_spmd.clone, body=%wide.region_0.2_spmd.clone.sunk | while | flops 202899920 | bytes 15731517 | solution.py:40
  244.0 9.3 %scatter_fusion = f32[8,16,128,128]{3,2,1,0:T(8,128)} fusion(f32[8,16,128,128]{3,2,1,0:T(8,128)} %get-tuple-element.132, s32[48]{0:T(128)S(1)} %reshape.119, f32[48,128,128]{2,1,0:T(8,128)S(1)} %bitcast.70), kind=kCustom, calls=%fused_computation.2.clone.clone.1 | custom fusion | flops 786432 | bytes 9437568 | tf_op jit(solution)/shard_map/while/body/eval_jaxpr/scatter-add | solution.py:38
  253.6 2.4 convolution_select_fusion.2
  256.0 9.3 %scatter_fusion = f32[8,16,128,128]{3,2,1,0:T(8,128)} fusion(f32[8,16,128,128]{3,2,1,0:T(8,128)} %get-tuple-element.132, s32[48]{0:T(128)S(1)} %reshape.119, f32[48,128,128]{2,1,0:T(8,128)S(1)} %bitcast.70), kind=kCustom, calls=%fused_computation.2.clone.clone.1 | custom fusion | flops 786432 | bytes 9437568 | tf_op jit(solution)/shard_map/while/body/eval_jaxpr/scatter-add | solution.py:38
  265.5 2.4 convolution_select_fusion.2
  268.0 9.3 %scatter_fusion = f32[8,16,128,128]{3,2,1,0:T(8,128)} fusion(f32[8,16,128,128]{3,2,1,0:T(8,128)} %get-tuple-element.132, s32[48]{0:T(128)S(1)} %reshape.119, f32[48,128,128]{2,1,0:T(8,128)S(1)} %bitcast.70), kind=kCustom, calls=%fused_computation.2.clone.clone.1 | custom fusion | flops 786432 | bytes 9437568 | tf_op jit(solution)/shard_map/while/body/eval_jaxpr/scatter-add | solution.py:38
  277.6 2.4 convolution_select_fusion.2
  280.0 9.3 %scatter_fusion = f32[8,16,128,128]{3,2,1,0:T(8,128)} fusion(f32[8,16,128,128]{3,2,1,0:T(8,128)} %get-tuple-element.132, s32[48]{0:T(128)S(1)} %reshape.119, f32[48,128,128]{2,1,0:T(8,128)S(1)} %bitcast.70), kind=kCustom, calls=%fused_computation.2.clone.clone.1 | custom fusion | flops 786432 | bytes 9437568 | tf_op jit(solution)/shard_map/while/body/eval_jaxpr/scatter-add | solution.py:38
  292.0 9.4 %scatter_fusion = f32[8,16,128,128]{3,2,1,0:T(8,128)} fusion(f32[8,16,128,128]{3,2,1,0:T(8,128)} %get-tuple-element.132, s32[48]{0:T(128)S(1)} %reshape.119, f32[48,128,128]{2,1,0:T(8,128)S(1)} %bitcast.70), kind=kCustom, calls=%fused_computation.2.clone.clone.1 | custom fusion | flops 786432 | bytes 9437568 | tf_op jit(solution)/shard_map/while/body/eval_jaxpr/scatter-add | solution.py:38
  301.6 2.4 convolution_select_fusion.2
  304.1 9.3 %scatter_fusion = f32[8,16,128,128]{3,2,1,0:T(8,128)} fusion(f32[8,16,128,128]{3,2,1,0:T(8,128)} %get-tuple-element.132, s32[48]{0:T(128)S(1)} %reshape.119, f32[48,128,128]{2,1,0:T(8,128)S(1)} %bitcast.70), kind=kCustom, calls=%fused_computation.2.clone.clone.1 | custom fusion | flops 786432 | bytes 9437568 | tf_op jit(solution)/shard_map/while/body/eval_jaxpr/scatter-add | solution.py:38
  313.7 2.4 convolution_select_fusion.2
  316.1 9.3 %scatter_fusion = f32[8,16,128,128]{3,2,1,0:T(8,128)} fusion(f32[8,16,128,128]{3,2,1,0:T(8,128)} %get-tuple-element.132, s32[48]{0:T(128)S(1)} %reshape.119, f32[48,128,128]{2,1,0:T(8,128)S(1)} %bitcast.70), kind=kCustom, calls=%fused_computation.2.clone.clone.1 | custom fusion | flops 786432 | bytes 9437568 | tf_op jit(solution)/shard_map/while/body/eval_jaxpr/scatter-add | solution.py:38
  328.1 9.3 %scatter_fusion = f32[8,16,128,128]{3,2,1,0:T(8,128)} fusion(f32[8,16,128,128]{3,2,1,0:T(8,128)} %get-tuple-element.132, s32[48]{0:T(128)S(1)} %reshape.119, f32[48,128,128]{2,1,0:T(8,128)S(1)} %bitcast.70), kind=kCustom, calls=%fused_computation.2.clone.clone.1 | custom fusion | flops 786432 | bytes 9437568 | tf_op jit(solution)/shard_map/while/body/eval_jaxpr/scatter-add | solution.py:38
  337.4 151.0 %reduce-scatter.2.cloned.1.call-done = f32[2,16,128,128]{3,2,1,0:T(8,128)} async-done(((f32[8,16,128,128]{3,2,1,0:T(8,128)}), f32[2,16,128,128]{3,2,1,0:T(8,128)}) %reduce-scatter.2.cloned.1.call-update) | async-done | bytes 2097168 | tf_op jit(solution)/shard_map/reduce_scatter | solution.py:67
  490.3 75.4 %psum.7 = f32[16,128]{1,0:T(8,128)S(1)} all-reduce(f32[16,128]{1,0:T(8,128)S(1)} %multiply_reduce_fusion), channel_id=1, replica_groups=mesh['row'=8,'col'=8,'fiber'=4] {'row','fiber'}, use_global_device_ids=true, to_apply=%region_5.6 | all-reduce | flops 2048 | bytes 16384 | tf_op jit(solution)/shard_map/psum | solution.py:69
  (83 shorter events, 15.3 us)
Async XLA Ops:
  6.5 25.3 %copy-start.4 = (u32[256]{0:T(256)S(1)}, u32[256]{0:T(256)}, u32[]{:S(2)}) copy-start(u32[256]{0:T(256)} %constant.138) | copy-start | bytes 3076
  6.5 1.5 copy-start.1
  6.5 26.5 %copy-start.3 = (s32[64,1]{0,1:T(1,128)S(1)}, s32[64,1]{0,1:T(1,128)}, u32[]{:S(2)}) copy-start(s32[64,1]{0,1:T(1,128)} %param.11) | copy-start | bytes 772
  6.5 94.5 %all-gather.7.cloned.1.call-start = ((), (), s32[]{:S(2)}) async-start(), calls=%async_computation.2 | async-start | bytes 18874368 | tf_op jit(solution)/shard_map/all_gather | solution.py:55
  7.3 43.5 %copy-start.2 = (s32[8,1]{0,1:T(1,128)S(1)}, s32[8,1]{0,1:T(1,128)}, u32[]{:S(2)}) copy-start(s32[8,1]{0,1:T(1,128)} %param.9) | copy-start | bytes 100
  7.3 229.8 %all-gather.5.cloned.1.call-start = ((), (), s32[]{:S(2)}) async-start(), calls=%async_computation.1 | async-start | bytes 14155776 | tf_op jit(solution)/shard_map/all_gather | solution.py:58
  8.0 480.4 %reduce-scatter.2.cloned.1.call-start = ((), (), s32[]{:S(2)}) async-start(), calls=%async_computation.3 | async-start | bytes 10485760 | tf_op jit(solution)/shard_map/reduce_scatter | solution.py:67
  488.4 77.3 %copy-start = (f32[2,16,128,128]{3,2,1,0:T(8,128)S(1)}, f32[2,16,128,128]{3,2,1,0:T(8,128)}, u32[]{:S(2)}) copy-start(f32[2,16,128,128]{3,2,1,0:T(8,128)} %reduce-scatter.2.cloned.1.call-done) | copy-start | bytes 6291460
Sparse Core Ops, SparseCore 0:
  9.2 91.7 all-gather.6
  102.8 134.1 all-gather.4
  337.5 150.8 reduce-scatter.1
where the time goes:
time: 577 us; the launch traced here: 574 us
  waiting for transfers between devices  303 us (53%)
  blocking collectives  128 us (22%)
  other arithmetic  78.5 us (14%)
  local copies, waits for them, and re-layouts  30.1 us (5%)
  matrix products  19.6 us (3%)
  between operations  13.8 us (2%)
    reduce_scatter x1, waiting for transfers between devices, on_device(): lax.psum_scatter(partial_value, 'fiber', scatter_dimension=0, tiled=True)  151 us
    all_gather x1, waiting for transfers between devices, on_device(): tile_set = lax.all_gather(a_tiles, 'col', axis=1, tiled=True)  115 us
    psum x1, blocking collectives, on_device(): column_total = lax.psum(jnp.sum(inflated, axis=(0, 2)), ('row', 'fiber'))  75.4 us
    scatter-add x8, other arithmetic, one_group(): return (carry.at[row_ids[:, None], group_target].add(products), None)  74.6 us
    all_gather x1, waiting for transfers between devices, on_device(): lax.all_gather(b_tiles, 'row', axis=0, tiled=True)  35.4 us
    all_gather x1, blocking collectives, on_device(): tile_cols = lax.all_gather(a_cols, 'col', axis=1, tiled=True)  23.5 us
    gather x1, local copies, waits for them, and re-layouts, on_device(): partner = panel_tiles[position, 0]  20.6 us
    dot_general x8, matrix products, one_group(): jnp.einsum('msab,msbc->msac', group_tiles, group_partner, preferred_eleme...  19.6 us
  transfers between devices with their start and end apart: 3, of which 3 were waited for; matrix products, arithmetic and copies ran while one was open for 4% of the time, Pallas kernels for 0%

commit v1 on v0

v1 whole, which is shorter than its diff:
```python
import functools

import jax
import jax.numpy as jnp
from jax import lax
from jax.experimental import pallas as pl
from jax.experimental.pallas import tpu as pltpu
from jax.sharding import PartitionSpec as P

MESH = pl.DeviceIdType.MESH
PT = 128
ASLOTS = 6
SLOTS8 = 8
TILE = 128
epsilon = 1e-06
F32 = jnp.float32
PIECES = 4
TOP = 32767.0


def kernel(total_rows, am_ref, bm_ref, a_ref, b_ref, out_ref, pa, pb, ma, mb, meta_v, meta_s, sums, cq_s, cs_s, cq_r, cs_r, own, t1, t2, gains,
           loc_sem, ma_sem, mb_sem, ao_sem, ap_sem, af_sem, bo_sem, bk_sem, bf_sem, cq_sem, cs_sem, t1_sem, t2_sem):
    r, c, f = lax.axis_index("row"), lax.axis_index("col"), lax.axis_index("fiber")
    x, k = r // 2, r % 2
    zl, y = c // 4, c % 4

    def rdev(rr):
        return (rr, c, f)

    def cdev(cc):
        return (r, cc, f)

    def fdev(ff):
        return (r, c, ff)

    def rid(dx, kk):
        return ((x + dx + 4) % 4) * 2 + kk

    def cid(dy, zz):
        return zz * 4 + (y + dy + 4) % 4

    XP, XM, KP = rdev(rid(1, k)), rdev(rid(-1, k)), rdev(rid(0, 1 - k))
    YP, YM, ZP = cdev(cid(1, zl)), cdev(cid(-1, zl)), cdev(cid(0, 1 - zl))
    FP, FM = fdev((f + 1) % 4), fdev((f + 3) % 4)
    row_peers = [rdev((r + d) % 8) for d in range(1, 8)]
    col_peers = [cdev((c + d) % 8) for d in range(1, 8)]
    fib_peers = [fdev((f + d) % 4) for d in range(1, 4)]

    barrier = pltpu.get_barrier_semaphore()
    for peer in row_peers + col_peers + fib_peers:
        pl.semaphore_signal(barrier, inc=1, device_id=peer, device_id_type=MESH)

    locals_ = [
        pltpu.make_async_copy(am_ref, ma.at[c], loc_sem.at[0]),
        pltpu.make_async_copy(bm_ref, mb.at[r], loc_sem.at[1]),
        pltpu.make_async_copy(a_ref, pa.at[:, c], loc_sem.at[2]),
        pltpu.make_async_copy(b_ref, pb.at[pl.ds(r * 64, 64)], loc_sem.at[3]),
    ]
    for copy in locals_:
        copy.start()
    sums[0] = jnp.zeros((TILE, TILE), F32)
    pl.semaphore_wait(barrier, len(row_peers) + len(col_peers) + len(fib_peers))

    started = []

    def send(src, dst, sem, at, device):
        copy = pltpu.make_async_remote_copy(
            src_ref=src, dst_ref=dst, send_sem=sem.at[(0,) + at], recv_sem=sem.at[(1,) + at], device_id=device, device_id_type=MESH
        )
        copy.start()
        started.append(copy)

    def arrive(dst, sem, at):
        pltpu.make_async_remote_copy(
            src_ref=dst, dst_ref=dst, send_sem=sem.at[(0,) + at], recv_sem=sem.at[(1,) + at], device_id=KP, device_id_type=MESH
        ).wait_recv()

    for d in range(1, 8):
        send(am_ref, ma.at[c], ma_sem, (d - 1,), col_peers[d - 1])
        send(bm_ref, mb.at[r], mb_sem, (d - 1,), row_peers[d - 1])

    step = 64 // PIECES

    def b_at(block, q):
        return pb.at[pl.ds(block * 64 + q * step, step)]

    for q in range(PIECES):
        src = b_ref.at[pl.ds(q * step, step)]
        send(src, b_at(r, q), bo_sem, (q, 1), XP)
        send(src, b_at(r, q), bo_sem, (q, 2), XM)
        send(src, b_at(r, q), bo_sem, (q, 0), KP)

    def b_near(q):
        block = rid(-1, k)
        arrive(b_at(block, q), bo_sem, (q, 1))
        if q < PIECES // 2:
            send(b_at(block, q), b_at(block, q), bf_sem, (q,), XP)
        send(b_at(block, q), b_at(block, q), bk_sem, (q, 0), KP)
        block = rid(1, k)
        arrive(b_at(block, q), bo_sem, (q, 2))
        if q >= PIECES // 2:
            send(b_at(block, q), b_at(block, q), bf_sem, (q,), XM)
        send(b_at(block, q), b_at(block, q), bk_sem, (q, 1), KP)

    def b_far(q):
        block = rid(2, k)
        arrive(b_at(block, q), bf_sem, (q,))
        send(b_at(block, q), b_at(block, q), bk_sem, (q, 2), KP)

    def b_done():
        for q in range(PIECES):
            arrive(b_at(rid(0, 1 - k), q), bo_sem, (q, 0))
            arrive(b_at(rid(-1, 1 - k), q), bk_sem, (q, 0))
            arrive(b_at(rid(1, 1 - k), q), bk_sem, (q, 1))
            arrive(b_at(rid(2, 1 - k), q), bk_sem, (q, 2))
        locals_[3].wait()

    plus, minus, far = (f + 1) % 4, (f + 3) % 4, (f + 2) % 4
    rows = [far * 2, far * 2 + 1, plus * 2 + 1, minus * 2, plus * 2, minus * 2 + 1, f * 2, f * 2 + 1]

    def a_own(n):
        row = rows[n]
        for way, device in enumerate((ZP, YP, YM)):
            send(a_ref.at[row], pa.at[row, c], ao_sem, (n, way), device)

    def a_half(n, block, half, way, device):
        part = pa.at[rows[n], block, pl.ds(half * 3, 3)]
        send(part, part, af_sem, (n, way), device)

    def a_near(n):
        row = rows[n]
        block = cid(0, 1 - zl)
        arrive(pa.at[row, block], ao_sem, (n, 0))
        for way, device in enumerate((YP, YM)):
            send(pa.at[row, block], pa.at[row, block], ap_sem, (n, way), device)
        if n + 2 < 8:
            a_own(n + 2)
        arrive(pa.at[row, cid(-1, zl)], ao_sem, (n, 1))
        a_half(n, cid(-1, zl), 0, 0, YP)
        arrive(pa.at[row, cid(1, zl)], ao_sem, (n, 2))
        a_half(n, cid(1, zl), 1, 1, YM)

    def a_pair(n):
        row = rows[n]
        arrive(pa.at[row, cid(-1, 1 - zl)], ap_sem, (n, 0))
        a_half(n, cid(-1, 1 - zl), 0, 2, YP)
        arrive(pa.at[row, cid(1, 1 - zl)], ap_sem, (n, 1))
        a_half(n, cid(1, 1 - zl), 1, 3, YM)

    def a_done(n):
        row = rows[n]
        for way, (zz, half) in enumerate(((zl, 0), (zl, 1), (1 - zl, 0), (1 - zl, 1))):
            arrive(pa.at[row, cid(2, zz), pl.ds(half * 3, 3)], af_sem, (n, way))

    def index_tables():
        locals_[0].wait()
        locals_[1].wait()
        for d in range(1, 8):
            arrive(ma.at[(c + 8 - d) % 8], ma_sem, (d - 1,))
            arrive(mb.at[(r + 8 - d) % 8], mb_sem, (d - 1,))
        lane = lax.broadcasted_iota(jnp.int32, (64, TILE), 1)
        slot = lax.broadcasted_iota(jnp.int32, (64, TILE), 0)

        def one_row(i, carry):
            place = ma[:, i].reshape(64, TILE)
            target = jnp.zeros((64, TILE), jnp.int32)
            for q in range(8):
                hit = (place == lane + q * 64) & (lane < 64)
                target = target + jnp.where(hit, mb[q, 0:1, :], 0)
            target = jnp.sum(target, axis=1, keepdims=True)
            target = jnp.broadcast_to(target, (64, TILE))
            here = slot == lane
            target_l = jnp.sum(jnp.where(here, target, 0), axis=0, keepdims=True)
            place_l = jnp.sum(jnp.where(here, jnp.maximum(place, 0), 0), axis=0, keepdims=True)
            same = (target == target_l) & (slot < lane) & (target > 0)
            prev = jnp.max(jnp.where(same, slot + 1, 0), axis=0, keepdims=True)
            last = jnp.max(jnp.where(target == lane + 1, slot + 1, 0), axis=0, keepdims=True)
            meta_v[i, 0:1, :] = place_l
            meta_v[i, 1:2, :] = prev
            meta_v[i, 2:3, :] = last
            return carry

        lax.fori_loop(0, 8, one_row, 0)
        copy = pltpu.make_async_copy(meta_v, meta_s, loc_sem.at[4])
        copy.start()
        copy.wait()
        locals_[2].wait()

    def products(n):
        row = rows[n]

        def one_part(p, carry):
            for e in range(ASLOTS):
                t = p * SLOTS8 + e
                product = jnp.dot(pa[row, p, e], pb[meta_s[row, 0, t]], preferred_element_type=F32)
                sums[1 + t] = product + sums[meta_s[row, 1, t]]
            return carry

        lax.fori_loop(0, 8, one_part, 0)

    def decoded(at, j):
        return cq_r[at, j].astype(jnp.int32).astype(F32) * cs_r[at, pl.ds(j, 1), :]

    def emit(n, at, device, add=None):
        row = rows[n]

        def one_tile(j, carry):
            value = sums[meta_s[row, 2, j]]
            if add is not None:
                value = value + decoded(add, j)
            top = jnp.max(jnp.abs(value), axis=0, keepdims=True)
            gain = jnp.where(top > 1e-30, TOP / jnp.maximum(top, 1e-30), 0.0)
            cs_s[at, pl.ds(j, 1), :] = top * (1.0 / TOP)
            cq_s[at, j] = jnp.floor(value * gain + 0.5).astype(jnp.int32).astype(jnp.int16)
            return carry

        lax.fori_loop(0, 16, one_tile, 0)
        send(cs_s.at[at], cs_r.at[at], cs_sem, (at,), device)
        send(cq_s.at[at], cq_r.at[at], cq_sem, (at,), device)

    def c_arrive(at):
        arrive(cs_r.at[at], cs_sem, (at,))
        arrive(cq_r.at[at], cq_sem, (at,))

    def keep(n, half):
        row = rows[n]

        def one_tile(j, carry):
            own[half, j] = sums[meta_s[row, 2, j]]
            return carry

        lax.fori_loop(0, 16, one_tile, 0)

    a_own(0)
    a_own(1)
    a_near(0)
    index_tables()
    b_near(0)
    a_near(1)
    a_pair(0)
    b_near(1)
    a_near(2)
    a_pair(1)
    b_near(2)
    a_near(3)
    a_pair(2)
    b_near(3)
    a_near(4)
    a_pair(3)
    b_far(0)
    b_far(2)
    a_near(5)
    a_pair(4)
    b_far(1)
    b_far(3)
    b_done()
    a_done(0)
    products(0)
    emit(0, 0, FP)
    a_near(6)
    a_pair(5)
    a_done(1)
    products(1)
    emit(1, 1, FM)
    a_done(2)
    products(2)
    emit(2, 3, FP)
    a_near(7)
    a_pair(6)
    a_done(3)
    products(3)
    emit(3, 4, FM)
    a_done(4)
    products(4)
    c_arrive(0)
    emit(4, 2, FP, add=0)
    a_pair(7)
    a_done(5)
    products(5)
    c_arrive(1)
    emit(5, 5, FM, add=1)
    a_done(6)
    products(6)
    keep(6, 0)
    a_done(7)
    products(7)
    keep(7, 1)
    for at in (3, 4, 2, 5):
        c_arrive(at)

    def square(j, carry):
        total = jnp.zeros((1, TILE), F32)
        for half in range(2):
            value = own[half, j] + decoded(2 + half, j) + decoded(4 + half, j)
            value = value * value
            own[half, j] = value
            total = total + jnp.sum(value, axis=0, keepdims=True)
        t1[r, pl.ds(j, 1), :] = total
        return carry

    lax.fori_loop(0, 16, square, 0)
    for d in range(1, 8):
        send(t1.at[r], t1.at[r], t1_sem, (d - 1,), row_peers[d - 1])
    for d in range(1, 8):
        arrive(t1.at[(r + 8 - d) % 8], t1_sem, (d - 1,))
    t2[f] = jnp.sum(t1[...], axis=0)
    for d in range(1, 4):
        send(t2.at[f], t2.at[f], t2_sem, (d - 1,), fib_peers[d - 1])
    for d in range(1, 4):
        arrive(t2.at[(f + 4 - d) % 4], t2_sem, (d - 1,))
    gains[...] = total_rows / (jnp.sum(t2[...], axis=0) + epsilon)

    def scale(j, carry):
        gain = gains[pl.ds(j, 1), :]
        for half in range(2):
            out_ref[half, j] = own[half, j] * gain
        return carry

    lax.fori_loop(0, 16, scale, 0)
    for copy in started:
        copy.wait_send()


def on_device(a_tiles, a_cols, a_count, b_tiles, b_cols):
    fibers = lax.axis_size("fiber")
    block_rows = b_tiles.shape[0]
    col_offset = lax.axis_index("col") * (PT // lax.axis_size("col"))
    place = a_cols // (block_rows * fibers) * block_rows + a_cols % block_rows
    place = jnp.where(jnp.arange(ASLOTS)[None, :] < a_count, place, -1)
    place = jnp.pad(place, ((0, 0), (0, SLOTS8 - ASLOTS)), constant_values=-1)
    place = jnp.broadcast_to(place[:, :, None], place.shape + (TILE,))
    target = jnp.pad(b_cols[:, 0] - col_offset + 1, (0, TILE - block_rows))
    target = jnp.broadcast_to(target[None, :], (8, TILE))
    total_rows = 8 * lax.axis_size("row") * TILE
    dma = pltpu.SemaphoreType.DMA
    any_ = pl.BlockSpec(memory_space=pl.ANY)
    return pl.pallas_call(
        functools.partial(kernel, total_rows),
        out_shape=jax.ShapeDtypeStruct((2, 16, TILE, TILE), F32),
        in_specs=[any_] * 4,
        out_specs=pl.BlockSpec(memory_space=pltpu.VMEM),
        scratch_shapes=[
            pltpu.VMEM((8, 8, ASLOTS, TILE, TILE), jnp.bfloat16),
            pltpu.VMEM((512, TILE, TILE), jnp.bfloat16),
            pltpu.VMEM((8, 8, SLOTS8, TILE), jnp.int32),
            pltpu.VMEM((8, 8, TILE), jnp.int32),
            pltpu.VMEM((8, 8, TILE), jnp.int32),
            pltpu.SMEM((8, 8, TILE), jnp.int32),
            pltpu.VMEM((65, TILE, TILE), F32),
            pltpu.VMEM((6, 16, TILE, TILE), jnp.int16),
            pltpu.VMEM((6, 16, TILE), F32),
            pltpu.VMEM((6, 16, TILE, TILE), jnp.int16),
            pltpu.VMEM((6, 16, TILE), F32),
            pltpu.VMEM((2, 16, TILE, TILE), F32),
            pltpu.VMEM((8, 16, TILE), F32),
            pltpu.VMEM((4, 16, TILE), F32),
            pltpu.VMEM((16, TILE), F32),
            dma((5,)),
            dma((2, 7)),
            dma((2, 7)),
            dma((2, 8, 3)),
            dma((2, 8, 2)),
            dma((2, 8, 4)),
            dma((2, PIECES, 3)),
            dma((2, PIECES, 3)),
            dma((2, PIECES)),
            dma((2, 6)),
            dma((2, 6)),
            dma((2, 7)),
            dma((2, 3)),
        ],
        compiler_params=pltpu.CompilerParams(collective_id=0, has_side_effects=True, vmem_limit_bytes=60 * 1024 * 1024),
    )(place, target, a_tiles, b_tiles.reshape(block_rows, TILE, TILE))


def solution(mesh):
    placed = (
        P("row", ("col", "fiber"), None, None),
        P("row", ("col", "fiber")),
        P("row", ("col", "fiber")),
        P(("row", "fiber"), "col", None, None),
        P(("row", "fiber"), "col"),
    )
    return jax.shard_map(
        on_device,
        mesh=mesh,
        in_specs=placed,
        out_specs=P(("row", "fiber"), "col", None, None),
        check_vma=False,
    )
```

time: 577 us -> 181 us (0.31)
  waiting for transfers between devices: 303 us -> 0 us
  Pallas kernels: 0 us -> 175 us
  blocking collectives: 128 us -> 0 us
  other arithmetic: 78.5 us -> 1.42 us
  local copies, waits for them, and re-layouts: 30.1 us -> 4.44 us
  matrix products: 19.6 us -> 0 us
  between operations: 13.8 us -> 0.01 us
    pallas_call x0 -> x1, Pallas kernels: none -> 175 us  [on_device(): pl.pallas_call(functools.partial(kernel, total_rows), out_shape=jax.Shape...]
    reduce_scatter x1 -> x0, waiting for transfers between devices: 151 us -> none  [on_device(): lax.psum_scatter(partial_value, 'fiber', scatter_dimension=0, tiled=True)]
    all_gather x2 -> x0, waiting for transfers between devices: 151 us -> none  [the longest x1 115 us: on_device(): tile_set = lax.all_gather(a_tiles, 'col', axis=1, tiled=True)]
    psum x1 -> x0, blocking collectives: 75.4 us -> none  [on_device(): column_total = lax.psum(jnp.sum(inflated, axis=(0, 2)), ('row', 'fiber'))]
    scatter-add x8 -> x0, other arithmetic: 74.6 us -> none  [one_group(): return (carry.at[row_ids[:, None], group_target].add(products), None)]
    all_gather x2 -> x0, blocking collectives: 38.3 us -> none  [the longest x1 23.5 us: on_device(): tile_cols = lax.all_gather(a_cols, 'col', axis=1, tiled=True)]
    gather x2 -> x0, local copies, waits for them, and re-layouts: 23.2 us -> none  [the longest x1 20.6 us: on_device(): partner = panel_tiles[position, 0]]
    dot_general x8 -> x0, matrix products: 19.6 us -> none  [one_group(): jnp.einsum('msab,msbc->msac', group_tiles, group_partner, preferred_eleme...]
  transfers between devices with their start and end apart: 3 -> 0, of which waited for: 3 -> 0; matrix products, arithmetic and copies ran while one was open for 4% -> 0% of each run, Pallas kernels for 0% -> 0%
where the time goes in v1:
time: 181 us
  Pallas kernels  175 us (97%)
  local copies, waits for them, and re-layouts  4.44 us (2%)
    pallas_call x1, Pallas kernels, on_device(): pl.pallas_call(functools.partial(kernel, total_rows), out_shape=jax.Shape...  175 us

profile of v1, /device:TPU:1, one launch (start us, length us, event | category | flops | bytes accessed | tf_op | source)
XLA Modules:
  0.0 180.9 jit_solution(3092168179069809508)
XLA Ops:
  0.0 0.7 add_bitcast_fusion
  0.7 0.6 broadcast_in_dim.7.bm_ref
  1.3 0.8 fusion.3
  2.0 0.7 broadcast_in_dim.6.am_ref
  2.7 175.0 %shard_map.55 = f32[2,16,128,128]{3,2,1,0:T(8,128)} custom-call(s32[8,8,128]{2,1,0:T(8,128)} %broadcast_in_dim.6.am_ref, s32[8,128]{1,0:T(8,128)} %broadcast_in_dim.7.bm_ref, bf16[8,6,128,128]{3,2,1,0:T(8,128)(2,1)} %a_ref.1, bf16[64,128,128]{2,1,0:T(8,128)(2,1)} %bitcast.4), custom_call_target="tpu_custom_call" | custom-call | tf_op jit(solution)/shard_map/pallas_call | solution.py:337
  177.7 3.1 %copy.7 = f32[2,16,128,128]{3,2,1,0:T(8,128)} copy(f32[2,16,128,128]{3,2,1,0:T(8,128)} %shard_map.55) | data formatting | bytes 4194304
  (2 shorter events, 0.0 us)

commit v2 on v1

v2 whole, which is shorter than its diff:
```python
import functools

import jax
import jax.numpy as jnp
from jax import lax
from jax.experimental import pallas as pl
from jax.experimental.pallas import tpu as pltpu
from jax.sharding import PartitionSpec as P

MESH = pl.DeviceIdType.MESH
PT = 128
ASLOTS = 6
SLOTS8 = 8
TILE = 128
epsilon = 1e-06
F32 = jnp.float32
PIECES = 4
TOP = 32767.0


def kernel(total_rows, meta_ref, a_ref, b_ref, out_ref, gain_ref, pa, pb0, pb1, raw, ma, mb, meta_v, meta_s, sums, cq_s, cs_s, cq_r, cs_r, own, t1, t2,
           loc_sem, ma_sem, mb_sem, ao_sem, ap_sem, af_sem, bo_sem, bk_sem, bf_sem, cq_sem, cs_sem, t1_sem, t2_sem):
    r, c, f = lax.axis_index("row"), lax.axis_index("col"), lax.axis_index("fiber")
    x, k = r // 2, r % 2
    zl, y = c // 4, c % 4
    pb = (pb0, pb1)

    def rdev(rr):
        return (rr, c, f)

    def cdev(cc):
        return (r, cc, f)

    def fdev(ff):
        return (r, c, ff)

    def rid(dx, kk):
        return ((x + dx + 4) % 4) * 2 + kk

    def cid(dy, zz):
        return zz * 4 + (y + dy + 4) % 4

    XP, XM, KP = rdev(rid(1, k)), rdev(rid(-1, k)), rdev(rid(0, 1 - k))
    YP, YM, ZP = cdev(cid(1, zl)), cdev(cid(-1, zl)), cdev(cid(0, 1 - zl))
    FP, FM = fdev((f + 1) % 4), fdev((f + 3) % 4)
    row_peers = [rdev((r + d) % 8) for d in range(1, 8)]
    col_peers = [cdev((c + d) % 8) for d in range(1, 8)]
    fib_peers = [fdev((f + d) % 4) for d in range(1, 4)]

    barrier = pltpu.get_barrier_semaphore()
    for peer in row_peers + col_peers + fib_peers:
        pl.semaphore_signal(barrier, inc=1, device_id=peer, device_id_type=MESH)

    am_ref, bm_ref = meta_ref.at[pl.ds(0, 8)], meta_ref.at[pl.ds(8, 8)]
    locals_ = [
        pltpu.make_async_copy(am_ref, ma.at[c], loc_sem.at[0]),
        pltpu.make_async_copy(bm_ref, mb.at[r], loc_sem.at[1]),
        pltpu.make_async_copy(a_ref, pa.at[:, c], loc_sem.at[2]),
        pltpu.make_async_copy(b_ref, raw, loc_sem.at[3]),
    ]
    for n in (3, 0, 1, 2):
        locals_[n].start()
    sums[0] = jnp.zeros((TILE, TILE), F32)
    low = lax.broadcasted_iota(jnp.int32, (1, TILE), 1) < TILE // 2

    def swapped(value):
        return pltpu.roll(value, TILE // 2, 1)

    def pack(h, q):
        def one_pair(n, carry):
            first, second = raw[2 * n].astype(F32), raw[2 * n + 1].astype(F32)
            if h == 0:
                pair = jnp.where(low, first, swapped(second))
            else:
                pair = jnp.where(low, swapped(first), second)
            pb[h][r * 32 + n] = pair.astype(jnp.bfloat16)
            return carry

        lax.fori_loop(q * (32 // PIECES), (q + 1) * (32 // PIECES), one_pair, 0)

    pl.semaphore_wait(barrier, len(row_peers) + len(col_peers) + len(fib_peers))

    started = []

    def send(src, dst, sem, at, device):
        copy = pltpu.make_async_remote_copy(
            src_ref=src, dst_ref=dst, send_sem=sem.at[(0,) + at], recv_sem=sem.at[(1,) + at], device_id=device, device_id_type=MESH
        )
        copy.start()
        started.append(copy)

    def arrive(dst, sem, at):
        pltpu.make_async_remote_copy(
            src_ref=dst, dst_ref=dst, send_sem=sem.at[(0,) + at], recv_sem=sem.at[(1,) + at], device_id=KP, device_id_type=MESH
        ).wait_recv()

    step = 32 // PIECES

    def b_at(h, block, q):
        return pb[h].at[pl.ds(block * 32 + q * step, step)]

    def b_own(h, q):
        part = b_at(h, r, q)
        send(part, part, bo_sem, (h, q, 1), XP)
        send(part, part, bo_sem, (h, q, 2), XM)
        send(part, part, bo_sem, (h, q, 0), KP)

    def b_near(h, q):
        part = b_at(h, rid(-1, k), q)
        arrive(part, bo_sem, (h, q, 1))
        if q < PIECES // 2:
            send(part, part, bf_sem, (h, q), XP)
        send(part, part, bk_sem, (h, q, 0), KP)
        part = b_at(h, rid(1, k), q)
        arrive(part, bo_sem, (h, q, 2))
        if q >= PIECES // 2:
            send(part, part, bf_sem, (h, q), XM)
        send(part, part, bk_sem, (h, q, 1), KP)

    def b_far(h, q):
        part = b_at(h, rid(2, k), q)
        arrive(part, bf_sem, (h, q))
        send(part, part, bk_sem, (h, q, 2), KP)

    def b_done(h):
        for q in range(PIECES):
            arrive(b_at(h, rid(0, 1 - k), q), bo_sem, (h, q, 0))
            arrive(b_at(h, rid(-1, 1 - k), q), bk_sem, (h, q, 0))
            arrive(b_at(h, rid(1, 1 - k), q), bk_sem, (h, q, 1))
            arrive(b_at(h, rid(2, 1 - k), q), bk_sem, (h, q, 2))

    plus, minus, far = (f + 1) % 4, (f + 3) % 4, (f + 2) % 4
    rows = [far * 2, far * 2 + 1, plus * 2 + 1, minus * 2, plus * 2, minus * 2 + 1, f * 2, f * 2 + 1]

    def a_own(n, ways):
        row = rows[n]
        for way, device in enumerate((ZP, YP, YM)):
            if way in ways:
                send(a_ref.at[row], pa.at[row, c], ao_sem, (n, way), device)

    def a_half(n, block, half, way, device):
        part = pa.at[rows[n], block, pl.ds(half * 3, 3)]
        send(part, part, af_sem, (n, way), device)

    def a_near(n):
        row = rows[n]
        block = cid(0, 1 - zl)
        arrive(pa.at[row, block], ao_sem, (n, 0))
        for way, device in enumerate((YP, YM)):
            send(pa.at[row, block], pa.at[row, block], ap_sem, (n, way), device)
        if n + 3 < 8:
            a_own(n + 3, (0,))
        arrive(pa.at[row, cid(-1, zl)], ao_sem, (n, 1))
        a_half(n, cid(-1, zl), 0, 0, YP)
        arrive(pa.at[row, cid(1, zl)], ao_sem, (n, 2))
        a_half(n, cid(1, zl), 1, 1, YM)

    def a_pair(n):
        row = rows[n]
        arrive(pa.at[row, cid(-1, 1 - zl)], ap_sem, (n, 0))
        a_half(n, cid(-1, 1 - zl), 0, 2, YP)
        arrive(pa.at[row, cid(1, 1 - zl)], ap_sem, (n, 1))
        a_half(n, cid(1, 1 - zl), 1, 3, YM)
        if n + 2 < 8:
            a_own(n + 2, (1, 2))

    def a_done(n):
        row = rows[n]
        for way, (zz, half) in enumerate(((zl, 0), (zl, 1), (1 - zl, 0), (1 - zl, 1))):
            arrive(pa.at[row, cid(2, zz), pl.ds(half * 3, 3)], af_sem, (n, way))

    def index_tables():
        for d in range(1, 8):
            arrive(ma.at[(c + 8 - d) % 8], ma_sem, (d - 1,))
            arrive(mb.at[(r + 8 - d) % 8], mb_sem, (d - 1,))
        lane = lax.broadcasted_iota(jnp.int32, (64, TILE), 1)
        slot = lax.broadcasted_iota(jnp.int32, (64, TILE), 0)
        lane8 = lax.broadcasted_iota(jnp.int32, (8, TILE), 1)
        slot8 = lax.broadcasted_iota(jnp.int32, (8, TILE), 0)

        def one_row(i, carry):
            place = []
            for p in range(8):
                part = jnp.broadcast_to(ma[p, pl.ds(i, 1), :], (8, TILE))
                part = jnp.sum(jnp.where(slot8 == lane8, part, 0), axis=1, keepdims=True)
                place.append(jnp.broadcast_to(part, (8, TILE)))
            place = jnp.concatenate(place, axis=0)
            target = jnp.zeros((64, TILE), jnp.int32)
            for q in range(8):
                hit = (place == lane + q * 64) & (lane < 64)
                target = target + jnp.where(hit, mb[q, 0:1, :], 0)
            target = jnp.sum(target, axis=1, keepdims=True)
            target = jnp.broadcast_to(target, (64, TILE))
            here = slot == lane
            target_l = jnp.sum(jnp.where(here, target, 0), axis=0, keepdims=True)
            place_l = jnp.sum(jnp.where(here, jnp.maximum(place, 0), 0), axis=0, keepdims=True)
            same = (target == target_l) & (slot < lane) & (target > 0)
            prev = jnp.max(jnp.where(same, slot + 1, 0), axis=0, keepdims=True)
            last = jnp.max(jnp.where(target == lane + 1, slot + 1, 0), axis=0, keepdims=True)
            meta_v[i, 0:1, :] = place_l >> 1
            meta_v[i, 1:2, :] = prev
            meta_v[i, 2:3, :] = last
            meta_v[i, 3:4, :] = place_l & 1
            return carry

        lax.fori_loop(0, 8, one_row, 0)
        copy = pltpu.make_async_copy(meta_v, meta_s, loc_sem.at[4])
        copy.start()
        copy.wait()

    def products(n, h):
        row = rows[n]
        half = lax.broadcasted_iota(jnp.int32, (1, TILE), 1) // (TILE // 2)

        def one_part(p, carry):
            for e in range(ASLOTS):
                t = p * SLOTS8 + e
                product = jnp.dot(pa[row, p, e], pb[h][meta_s[row, 0, t]], preferred_element_type=F32)
                product = jnp.where(half == meta_s[row, 3, t], product, 0.0)
                sums[1 + t] = product + sums[meta_s[row, 1, t]]
            return carry

        lax.fori_loop(0, 8, one_part, 0)

    def total_pair(row, n):
        first, second = sums[meta_s[row, 2, 2 * n]], sums[meta_s[row, 2, 2 * n + 1]]
        return jnp.where(low, first, second) + swapped(jnp.where(low, second, first))

    def decoded(at, n):
        return cq_r[at, n].astype(jnp.int32).astype(F32) * cs_r[at, pl.ds(n, 1), :]

    def emit(n, h, at, device, add=None):
        row = rows[n]
        at = at * 2 + h

        def one_tile(j, carry):
            value = total_pair(row, j)
            if add is not None:
                value = value + decoded(add * 2 + h, j)
            top = jnp.max(jnp.abs(value), axis=0, keepdims=True)
            gain = jnp.where(top > 1e-30, TOP / jnp.maximum(top, 1e-30), 0.0)
            cs_s[at, pl.ds(j, 1), :] = top * (1.0 / TOP)
            cq_s[at, j] = jnp.floor(value * gain + 0.5).astype(jnp.int32).astype(jnp.int16)
            return carry

        lax.fori_loop(0, 8, one_tile, 0)
        send(cs_s.at[at], cs_r.at[at], cs_sem, (at,), device)
        send(cq_s.at[at], cq_r.at[at], cq_sem, (at,), device)

    def c_arrive(at, h):
        at = at * 2 + h
        arrive(cs_r.at[at], cs_sem, (at,))
        arrive(cq_r.at[at], cq_sem, (at,))

    def keep(n, h, half):
        row = rows[n]

        def one_tile(j, carry):
            own[half, h, j] = total_pair(row, j)
            return carry

        lax.fori_loop(0, 8, one_tile, 0)

    def unit(n, h):
        products(n, h)
        if n == 0:
            emit(0, h, 0, FP)
        elif n == 1:
            emit(1, h, 1, FM)
        elif n == 2:
            emit(2, h, 3, FP)
        elif n == 3:
            emit(3, h, 4, FM)
        elif n == 4:
            c_arrive(0, h)
            emit(4, h, 2, FP, add=0)
        elif n == 5:
            c_arrive(1, h)
            emit(5, h, 5, FM, add=1)
        else:
            keep(n, h, n - 6)

    def start():
        for copy in locals_[:2]:
            copy.wait()
        for d in range(1, 8):
            send(ma.at[c], ma.at[c], ma_sem, (d - 1,), col_peers[d - 1])
            send(mb.at[r], mb.at[r], mb_sem, (d - 1,), row_peers[d - 1])
        a_own(0, (0, 1, 2))
        a_own(1, (0, 1, 2))
        a_own(2, (0,))
        locals_[3].wait()
        for q in range(PIECES):
            pack(0, q)
            b_own(0, q)
        for q in range(PIECES):
            pack(1, q)

    start()
    b_near(0, 0)
    a_near(0)
    a_near(1)
    b_near(0, 1)
    a_pair(0)
    index_tables()
    b_near(0, 2)
    a_pair(1)
    b_near(0, 3)
    a_near(2)
    b_far(0, 0)
    b_far(0, 2)
    b_own(1, 0)
    b_far(0, 1)
    b_far(0, 3)
    for q in range(1, PIECES):
        b_own(1, q)
    a_near(3)
    locals_[2].wait()
    b_done(0)
    a_done(0)
    unit(0, 0)
    a_pair(2)
    a_done(1)
    unit(1, 0)
    b_near(1, 0)
    a_pair(3)
    b_near(1, 1)
    a_done(2)
    unit(2, 0)
    b_near(1, 2)
    a_near(4)
    a_done(3)
    unit(3, 0)
    b_near(1, 3)
    a_near(5)
    b_far(1, 0)
    b_far(1, 2)
    a_pair(4)
    b_far(1, 1)
    b_far(1, 3)
    b_done(1)
    unit(0, 1)
    unit(1, 1)
    a_pair(5)
    unit(2, 1)
    unit(3, 1)
    a_done(4)
    unit(4, 0)
    a_near(6)
    a_done(5)
    unit(5, 0)
    a_near(7)
    unit(4, 1)
    unit(5, 1)
    a_pair(6)
    a_pair(7)
    a_done(6)
    unit(6, 0)
    unit(6, 1)
    a_done(7)
    unit(7, 0)
    unit(7, 1)

    def sums_in():
        for at in (3, 4, 2, 5):
            for h in range(2):
                c_arrive(at, h)

    sums_in()

    def square(j, carry):
        total = [jnp.zeros((1, TILE), F32)] * 2
        for half in range(2):
            pair = []
            for h in range(2):
                value = own[half, h, j] + decoded((2 + half) * 2 + h, j) + decoded((4 + half) * 2 + h, j)
                value = value * value
                total[h] = total[h] + jnp.sum(value, axis=0, keepdims=True)
                pair.append(value)
            out_ref[half, 2 * j] = jnp.where(low, pair[0], swapped(pair[1]))
            out_ref[half, 2 * j + 1] = jnp.where(low, swapped(pair[0]), pair[1])
        t1[r, pl.ds(2 * j, 1), :] = jnp.where(low, total[0], swapped(total[1]))
        t1[r, pl.ds(2 * j + 1, 1), :] = jnp.where(low, swapped(total[0]), total[1])
        return carry

    def squares():
        lax.fori_loop(0, 8, square, 0)

    def row_exchange():
        for d in range(1, 8):
            send(t1.at[r], t1.at[r], t1_sem, (d - 1,), row_peers[d - 1])
        for d in range(1, 8):
            arrive(t1.at[(r + 8 - d) % 8], t1_sem, (d - 1,))
        t2[f] = jnp.sum(t1[...], axis=0)

    def layer_exchange():
        for d in range(1, 4):
            send(t2.at[f], t2.at[f], t2_sem, (d - 1,), fib_peers[d - 1])
        for d in range(1, 4):
            arrive(t2.at[(f + 4 - d) % 4], t2_sem, (d - 1,))
        gain_ref[...] = total_rows / (jnp.sum(t2[...], axis=0) + epsilon)

    def last_waits():
        for copy in started:
            copy.wait_send()

    squares()
    row_exchange()
    layer_exchange()
    last_waits()


def on_device(a_tiles, a_cols, a_count, b_tiles, b_cols):
    fibers = lax.axis_size("fiber")
    block_rows = b_tiles.shape[0]
    col_offset = lax.axis_index("col") * (PT // lax.axis_size("col"))
    place = a_cols // (block_rows * fibers) * block_rows + a_cols % block_rows
    place = jnp.where(jnp.arange(ASLOTS)[None, :] < a_count, place, -1)
    place = jnp.pad(place, ((0, 8), (0, SLOTS8 - ASLOTS)), constant_values=-1)
    place = jnp.pad(place, ((0, 0), (0, TILE - SLOTS8)))
    target = jnp.pad((b_cols[:, 0] - col_offset + 1)[None, :], ((8, 7), (0, TILE - block_rows)))
    meta = jnp.where(jnp.arange(16)[:, None] < 8, place, target)
    total_rows = 8 * lax.axis_size("row") * TILE
    dma = pltpu.SemaphoreType.DMA
    any_ = pl.BlockSpec(memory_space=pl.ANY)
    squares, gains = pl.pallas_call(
        functools.partial(kernel, total_rows),
        out_shape=(pltpu.VMEM((2, 16, TILE, TILE), F32), pltpu.VMEM((16, TILE), F32)),
        in_specs=[any_] * 3,
        out_specs=(pl.BlockSpec(memory_space=pltpu.VMEM),) * 2,
        scratch_shapes=[
            pltpu.VMEM((8, 8, ASLOTS, TILE, TILE), jnp.bfloat16),
            pltpu.VMEM((256, TILE, TILE), jnp.bfloat16),
            pltpu.VMEM((256, TILE, TILE), jnp.bfloat16),
            pltpu.VMEM((64, TILE, TILE), jnp.bfloat16),
            pltpu.VMEM((8, 8, TILE), jnp.int32),
            pltpu.VMEM((8, 8, TILE), jnp.int32),
            pltpu.VMEM((8, 8, TILE), jnp.int32),
            pltpu.SMEM((8, 8, TILE), jnp.int32),
            pltpu.VMEM((65, TILE, TILE), F32),
            pltpu.VMEM((12, 8, TILE, TILE), jnp.int16),
            pltpu.VMEM((12, 8, TILE), F32),
            pltpu.VMEM((12, 8, TILE, TILE), jnp.int16),
            pltpu.VMEM((12, 8, TILE), F32),
            pltpu.VMEM((2, 2, 8, TILE, TILE), F32),
            pltpu.VMEM((8, 16, TILE), F32),
            pltpu.VMEM((4, 16, TILE), F32),
            dma((5,)),
            dma((2, 7)),
            dma((2, 7)),
            dma((2, 8, 3)),
            dma((2, 8, 2)),
            dma((2, 8, 4)),
            dma((2, 2, PIECES, 3)),
            dma((2, 2, PIECES, 3)),
            dma((2, 2, PIECES)),
            dma((2, 12)),
            dma((2, 12)),
            dma((2, 7)),
            dma((2, 3)),
        ],
        compiler_params=pltpu.CompilerParams(collective_id=0, has_side_effects=True, vmem_limit_bytes=56 * 1024 * 1024),
    )(meta, a_tiles, b_tiles.reshape(block_rows, TILE, TILE))
    return squares * gains[None, :, None, :]


def solution(mesh):
    placed = (
        P("row", ("col", "fiber"), None, None),
        P("row", ("col", "fiber")),
        P("row", ("col", "fiber")),
        P(("row", "fiber"), "col", None, None),
        P(("row", "fiber"), "col"),
    )
    return jax.shard_map(
        on_device,
        mesh=mesh,
        in_specs=placed,
        out_specs=P(("row", "fiber"), "col", None, None),
        check_vma=False,
    )
```

time: 181 us -> 150 us (0.83)
  Pallas kernels: 175 us -> 146 us
  local copies, waits for them, and re-layouts: 4.44 us -> 0 us
  other arithmetic: 1.42 us -> 3.67 us
    pallas_call x1, Pallas kernels: 175 us -> 146 us  [on_device(): pl.pallas_call(functools.partial(kernel, total_rows), out_shape=(pltpu.VM...]
    unnamed x1 -> x0, local copies, waits for them, and re-layouts: 3.14 us -> none
where the time goes in v2:
time: 150 us
  Pallas kernels  146 us (97%)
  other arithmetic  3.67 us (2%)
    pallas_call x1, Pallas kernels, on_device(): pl.pallas_call(functools.partial(kernel, total_rows), out_shape=(pltpu.VM...  146 us

profile of v2, /device:TPU:1, one launch (start us, length us, event | category | flops | bytes accessed | tf_op | source)
XLA Modules:
  0.0 149.8 jit_solution(951401039980933365)
XLA Ops:
  0.0 0.7 add_bitcast_fusion
  0.7 0.8 fusion.3
  1.4 0.7 select_select_fusion.meta_ref
  2.1 146.1 %shard_map.55 = (f32[2,16,128,128]{3,2,1,0:T(8,128)S(1)}, f32[16,128]{1,0:T(8,128)S(1)}) custom-call(s32[16,128]{1,0:T(8,128)} %select_select_fusion.meta_ref, bf16[8,6,128,128]{3,2,1,0:T(8,128)(2,1)} %a_ref.1, bf16[64,128,128]{2,1,0:T(8,128)(2,1)} %bitcast.4), custom_call_target="tpu_custom_call" | custom-call | tf_op jit(solution)/shard_map/pallas_call | solution.py:426
  148.2 1.6 %broadcast_multiply_fusion = f32[2,16,128,128]{3,2,1,0:T(8,128)} fusion(f32[2,16,128,128]{3,2,1,0:T(8,128)S(1)} %get-tuple-element.7, f32[16,128]{1,0:T(8,128)S(1)} %get-tuple-element.8), kind=kLoop, calls=%fused_computation | loop fusion | flops 524288 | bytes 4202496 | tf_op jit(solution)/shard_map/mul | solution.py:464
  (1 shorter events, 0.0 us)

commit v3 on v2

v3 whole, which is shorter than its diff:
```python
import functools

import jax
import jax.numpy as jnp
from jax import lax
from jax.experimental import pallas as pl
from jax.experimental.pallas import tpu as pltpu
from jax.sharding import PartitionSpec as P

MESH = pl.DeviceIdType.MESH
PT = 128
ASLOTS = 6
SLOTS8 = 8
TILE = 128
epsilon = 1e-06
F32 = jnp.float32
PIECES = 4
PARTS = 4
WIDE = TILE // PARTS
TOP = 32767.0


def kernel(total_rows, fibers, cols_ref, count_ref, target_ref, a_ref, b_ref, out_ref, gain_ref, pa, pb0, pb1, pb2, pb3, raw_b, ma, mn, mb, meta_v, meta_s, sums, cq_s, cs_s, cq_r, cs_r, own,
           t1, t2, loc_sem, ma_sem, mn_sem, mb_sem, ao_sem, ap_sem, af_sem, bo_sem, bk_sem, bf_sem, cq_sem, cs_sem, t1_sem, t2_sem):
    r, c, f = lax.axis_index("row"), lax.axis_index("col"), lax.axis_index("fiber")
    x, k = r // 2, r % 2
    zl, y = c // 4, c % 4
    pb = (pb0, pb1, pb2, pb3)

    def rdev(rr):
        return (rr, c, f)

    def cdev(cc):
        return (r, cc, f)

    def fdev(ff):
        return (r, c, ff)

    def rid(dx, kk):
        return ((x + dx + 4) % 4) * 2 + kk

    def cid(dy, zz):
        return zz * 4 + (y + dy + 4) % 4

    XP, XM, KP = rdev(rid(1, k)), rdev(rid(-1, k)), rdev(rid(0, 1 - k))
    YP, YM, ZP = cdev(cid(1, zl)), cdev(cid(-1, zl)), cdev(cid(0, 1 - zl))
    plus, minus, far = (f + 3 + 2 * zl) % 4, (f + 1 + 2 * zl) % 4, (f + 2) % 4
    FP, FM = fdev(plus), fdev(minus)
    row_peers = [rdev((r + d) % 8) for d in range(1, 8)]
    col_peers = [cdev((c + d) % 8) for d in range(1, 8)]
    fib_peers = [fdev((f + d) % 4) for d in range(1, 4)]

    barrier = pltpu.get_barrier_semaphore()
    for peer in row_peers + col_peers + fib_peers:
        pl.semaphore_signal(barrier, inc=1, device_id=peer, device_id_type=MESH)

    piece = 64 // PIECES
    locals_ = [
        pltpu.make_async_copy(cols_ref, ma.at[c], loc_sem.at[0]),
        pltpu.make_async_copy(target_ref, mb.at[r], loc_sem.at[1]),
        pltpu.make_async_copy(a_ref, pa.at[:, c], loc_sem.at[2]),
    ]
    for q in range(PIECES):
        part = pl.ds(q * piece, piece)
        locals_.append(pltpu.make_async_copy(b_ref.at[part], raw_b.at[part], loc_sem.at[4 + q]))
    locals_.append(pltpu.make_async_copy(count_ref, mn.at[c], loc_sem.at[4 + PIECES]))
    for copy in locals_:
        copy.start()
    for q in range(3 * PARTS):
        sums[q, 0] = jnp.zeros((WIDE, TILE), F32)

    sum_set = (0, 0, 0, 0, 1, 2, 0, 1)
    started = []

    def send(src, dst, sem, at, device):
        copy = pltpu.make_async_remote_copy(
            src_ref=src, dst_ref=dst, send_sem=sem.at[(0,) + at], recv_sem=sem.at[(1,) + at], device_id=device, device_id_type=MESH
        )
        copy.start()
        started.append(copy)

    def arrive(dst, sem, at):
        pltpu.make_async_remote_copy(
            src_ref=dst, dst_ref=dst, send_sem=sem.at[(0,) + at], recv_sem=sem.at[(1,) + at], device_id=KP, device_id_type=MESH
        ).wait_recv()

    def flip_b(q):
        def one_tile(n, carry):
            tile = raw_b[n].T
            for h in range(PARTS):
                pb[h][r * 64 + n] = tile[h * WIDE : (h + 1) * WIDE]
            return carry

        locals_[3 + q].wait()
        lax.fori_loop(q * piece, (q + 1) * piece, one_tile, 0)

    def b_at(h, block, q):
        return pb[h].at[pl.ds(block * 64 + q * piece, piece)]

    def b_own(h, q):
        part = b_at(h, r, q)
        send(part, part, bo_sem, (h, q, 1), XP)
        send(part, part, bo_sem, (h, q, 2), XM)
        send(part, part, bo_sem, (h, q, 0), KP)

    def b_all(h):
        for q in range(PIECES):
            b_own(h, q)

    def b_near(h, q):
        part = b_at(h, rid(-1, k), q)
        arrive(part, bo_sem, (h, q, 1))
        if q < PIECES // 2:
            send(part, part, bf_sem, (h, q), XP)
        send(part, part, bk_sem, (h, q, 0), KP)
        part = b_at(h, rid(1, k), q)
        arrive(part, bo_sem, (h, q, 2))
        if q >= PIECES // 2:
            send(part, part, bf_sem, (h, q), XM)
        send(part, part, bk_sem, (h, q, 1), KP)

    def b_far(h, q):
        for at in (q, q + PIECES // 2):
            part = b_at(h, rid(2, k), at)
            arrive(part, bf_sem, (h, at))
            send(part, part, bk_sem, (h, at, 2), KP)

    def b_done(h):
        for q in range(PIECES):
            arrive(b_at(h, rid(0, 1 - k), q), bo_sem, (h, q, 0))
            arrive(b_at(h, rid(-1, 1 - k), q), bk_sem, (h, q, 0))
            arrive(b_at(h, rid(1, 1 - k), q), bk_sem, (h, q, 1))
            arrive(b_at(h, rid(2, 1 - k), q), bk_sem, (h, q, 2))

    rows = [far * 2, far * 2 + 1, plus * 2 + 1, minus * 2, plus * 2, minus * 2 + 1, f * 2, f * 2 + 1]
    pair_rows = [far * 2, far * 2 + 1, minus * 2 + 1, plus * 2, minus * 2, plus * 2 + 1, f * 2, f * 2 + 1]

    def a_own(n, ways):
        for way, device in enumerate((ZP, YP, YM)):
            row = rows[n] if way else pair_rows[n]
            if way in ways:
                send(a_ref.at[row], pa.at[row, c], ao_sem, (n, way), device)

    def a_half(n, block, half, way, device):
        part = pa.at[rows[n], block, pl.ds(half * 3, 3)]
        send(part, part, af_sem, (n, way), device)

    def a_near(n):
        row = rows[n]
        block = cid(0, 1 - zl)
        arrive(pa.at[row, block], ao_sem, (n, 0))
        for way, device in enumerate((YP, YM)):
            send(pa.at[row, block], pa.at[row, block], ap_sem, (n, way), device)
        arrive(pa.at[row, cid(-1, zl)], ao_sem, (n, 1))
        a_half(n, cid(-1, zl), 0, 0, YP)
        arrive(pa.at[row, cid(1, zl)], ao_sem, (n, 2))
        a_half(n, cid(1, zl), 1, 1, YM)
        if n < 2:
            for later in range(3 + n * 3, min(6 + n * 3, 8)):
                a_own(later, (0,))

    def a_pair(n):
        row = rows[n]
        arrive(pa.at[row, cid(-1, 1 - zl)], ap_sem, (n, 0))
        a_half(n, cid(-1, 1 - zl), 0, 2, YP)
        arrive(pa.at[row, cid(1, 1 - zl)], ap_sem, (n, 1))
        a_half(n, cid(1, 1 - zl), 1, 3, YM)
        if n + 2 < 8:
            a_own(n + 2, (1, 2))

    def a_done(n):
        row = rows[n]
        for way, (zz, half) in enumerate(((zl, 0), (zl, 1), (1 - zl, 0), (1 - zl, 1))):
            arrive(pa.at[row, cid(2, zz), pl.ds(half * 3, 3)], af_sem, (n, way))

    def block_of(o):
        return ((zl + o) % 2) * 4 + (y + o // 2 + 3) % 4

    def index_tables():
        for d in range(1, 8):
            arrive(ma.at[(c + 8 - d) % 8], ma_sem, (d - 1,))
            arrive(mn.at[(c + 8 - d) % 8], mn_sem, (d - 1,))
            arrive(mb.at[(r + 8 - d) % 8], mb_sem, (d - 1,))
        lane = lax.broadcasted_iota(jnp.int32, (64, TILE), 1)
        slot = lax.broadcasted_iota(jnp.int32, (64, TILE), 0)
        kept = slot - (SLOTS8 - ASLOTS) * (slot // SLOTS8) + 1
        lane6 = lax.broadcasted_iota(jnp.int32, (8, ASLOTS), 1)
        slot6 = lax.broadcasted_iota(jnp.int32, (8, ASLOTS), 0)
        lane_n = lax.broadcasted_iota(jnp.int32, (1, 8), 1)

        def one_row(i, carry):
            place = []
            for o in range(8):
                block = block_of(o)
                part = jnp.broadcast_to(ma[block, pl.ds(i, 1), :], (8, ASLOTS))
                part = jnp.sum(jnp.where(slot6 == lane6, part, 0), axis=1, keepdims=True)
                live = jnp.sum(jnp.where(lane_n == i, mn[block], 0), axis=1, keepdims=True)
                part = jnp.broadcast_to(part, (8, TILE))
                part = part // (64 * fibers) * 64 + part % 64
                live = slot[:8] < jnp.broadcast_to(live, (8, TILE))
                place.append(jnp.where(live, part, -1))
            place = jnp.concatenate(place, axis=0)
            target = jnp.zeros((64, 64), jnp.int32)
            for q in range(8):
                hit = place[:, :64] == lane[:, :64] + q * 64
                target = target + jnp.where(hit, mb[q] - c * 16 + 1, 0)
            target = jnp.sum(target, axis=1, keepdims=True)
            target = jnp.broadcast_to(target, (64, TILE))
            here = slot == lane
            target_l = jnp.sum(jnp.where(here, target, 0), axis=0, keepdims=True)
            place_l = jnp.sum(jnp.where(here, jnp.maximum(place, 0), 0), axis=0, keepdims=True)
            same = (target == target_l) & (slot < lane) & (target > 0)
            prev = jnp.max(jnp.where(same, kept, 0), axis=0, keepdims=True)
            last = jnp.max(jnp.where(target == lane + 1, kept, 0), axis=0, keepdims=True)
            meta_v[i, 0:1, :] = place_l
            meta_v[i, 1:2, :] = prev
            meta_v[i, 2:3, :] = last
            return carry

        lax.fori_loop(0, 8, one_row, 0)
        copy = pltpu.make_async_copy(meta_v, meta_s, loc_sem.at[3])
        copy.start()
        copy.wait()
        locals_[2].wait()

    def products(n, parts, first=0, stop=8):
        row = rows[n]
        into = PARTS * sum_set[n]

        def one_block(o, carry):
            block = block_of(o)
            for e in range(ASLOTS):
                t = o * SLOTS8 + e
                place, prev = meta_s[row, 0, t], meta_s[row, 1, t]
                left = jnp.concatenate([pb[h][place] for h in parts], axis=0)
                product = lax.dot_general(left, pa[row, block, e], (((1,), (1,)), ((), ())), preferred_element_type=F32)
                for n_h, h in enumerate(parts):
                    sums[into + h, 1 + o * ASLOTS + e] = product[n_h * WIDE : (n_h + 1) * WIDE] + sums[into + h, prev]
            return carry

        lax.fori_loop(first, stop, one_block, 0)

    wide_lane = lax.broadcasted_iota(jnp.int32, (WIDE, TILE), 1)
    wide_slot = lax.broadcasted_iota(jnp.int32, (WIDE, TILE), 0)

    def to_lanes(column, i):
        return jnp.sum(jnp.where(wide_lane == wide_slot + i * WIDE, column, 0.0), axis=0, keepdims=True)

    def to_column(row, i):
        return jnp.sum(jnp.where(wide_lane == wide_slot + i * WIDE, row, 0.0), axis=1, keepdims=True)

    def decoded(at, g, i):
        return cq_r[at, g * 4 + i].astype(jnp.int32).astype(F32) * to_column(cs_r[at, pl.ds(g, 1), :], i)

    def emit(n, h, at, device, add=None):
        row = rows[n]
        at = at * PARTS + h

        def four_tiles(g, carry):
            scales = jnp.zeros((1, TILE), F32)
            for i in range(4):
                value = sums[PARTS * sum_set[n] + h, meta_s[row, 2, g * 4 + i]]
                if add is not None:
                    value = value + decoded(add * PARTS + h, g, i)
                top = jnp.max(jnp.abs(value), axis=1, keepdims=True)
                gain = jnp.where(top > 1e-30, TOP / jnp.maximum(top, 1e-30), 0.0)
                cq_s[at, g * 4 + i] = jnp.floor(value * gain + 0.5).astype(jnp.int32).astype(jnp.int16)
                scales = scales + to_lanes(top * (1.0 / TOP), i)
            cs_s[at, pl.ds(g, 1), :] = scales
            return carry

        lax.fori_loop(0, 4, four_tiles, 0)
        send(cs_s.at[at], cs_r.at[at], cs_sem, (at,), device)
        send(cq_s.at[at], cq_r.at[at], cq_sem, (at,), device)

    def c_arrive(at, h):
        at = at * PARTS + h
        arrive(cs_r.at[at], cs_sem, (at,))
        arrive(cq_r.at[at], cq_sem, (at,))

    def gather(h):
        for at in (3, 4, 2, 5):
            c_arrive(at, h)

        def four_tiles(g, carry):
            for i in range(4):
                for half in range(2):
                    own[half, h, g * 4 + i] = decoded((2 + half) * PARTS + h, g, i) + decoded((4 + half) * PARTS + h, g, i)
            return carry

        lax.fori_loop(0, 4, four_tiles, 0)

    def finish(n, h):
        row = rows[n]

        def four_tiles(g, carry):
            for i in range(4):
                j = g * 4 + i
                value = own[n - 6, h, j] + sums[PARTS * sum_set[n] + h, meta_s[row, 2, j]]
                value = value * value
                own[n - 6, h, j] = value
                total = to_lanes(jnp.sum(value, axis=1, keepdims=True), h)
                if (n, h) != (6, 0):
                    total = total + t1[r, pl.ds(j, 1), :]
                t1[r, pl.ds(j, 1), :] = total
            return carry

        lax.fori_loop(0, 4, four_tiles, 0)

    slots = ((0, FP, None), (1, FM, None), (3, FP, None), (4, FM, None), (2, FP, 0), (5, FM, 1))

    def give(n, h):
        at, device, add = slots[n]
        if add is not None:
            c_arrive(add, h)
        emit(n, h, at, device, add)

    def unit(n, *parts):
        products(n, parts)
        for h in parts:
            give(n, h)

    every = tuple(range(PARTS))

    def start():
        flip_b(0)
        pl.semaphore_wait(barrier, len(row_peers) + len(col_peers) + len(fib_peers))
        a_own(0, (0, 1, 2))
        b_own(0, 0)
        for n in (0, 1, -1):
            locals_[n].wait()
        for d in range(1, 8):
            send(ma.at[c], ma.at[c], ma_sem, (d - 1,), col_peers[d - 1])
            send(mn.at[c], mn.at[c], mn_sem, (d - 1,), col_peers[d - 1])
            send(mb.at[r], mb.at[r], mb_sem, (d - 1,), row_peers[d - 1])

    def start_b():
        flip_b(1)
        b_own(0, 1)
        a_own(1, (0, 1, 2))
        flip_b(2)
        b_own(0, 2)
        a_own(2, (0,))
        flip_b(3)
        b_own(0, 3)

    def last_waits():
        for copy in started:
            copy.wait_send()
        started.clear()

    start()
    start_b()
    b_near(0, 0)
    a_near(0)
    b_near(0, 1)
    b_near(0, 2)
    b_near(0, 3)
    b_all(1)
    a_pair(0)
    a_near(1)
    index_tables()
    b_far(0, 0)
    b_far(0, 1)
    b_done(0)
    a_done(0)
    unit(0, 0)
    b_near(1, 0)
    b_near(1, 1)
    a_pair(1)
    a_near(2)
    b_near(1, 2)
    b_near(1, 3)
    b_all(2)
    a_done(1)
    unit(1, 0)
    b_far(1, 0)
    b_far(1, 1)
    b_done(1)
    a_pair(2)
    a_near(3)
    unit(0, 1)
    b_near(2, 0)
    unit(1, 1)
    b_near(2, 1)
    b_near(2, 2)
    a_done(2)
    unit(2, 0, 1)
    b_near(2, 3)
    b_all(3)
    b_far(2, 0)
    a_pair(3)
    a_near(4)
    b_far(2, 1)
    b_done(2)
    unit(1, 2)
    unit(0, 2)
    b_near(3, 0)
    b_near(3, 1)
    a_done(3)
    unit(3, 0, 1)
    a_pair(4)
    a_near(5)
    b_near(3, 2)
    unit(2, 2)
    b_near(3, 3)
    unit(3, 2)
    a_done(4)
    products(4, (0, 1, 2))
    give(4, 0)
    b_far(3, 0)
    b_far(3, 1)
    b_done(3)
    unit(1, 3)
    unit(0, 3)
    a_pair(5)
    a_near(6)
    give(4, 1)
    unit(3, 3)
    a_done(5)
    products(5, every)
    give(5, 0)
    give(4, 2)
    give(5, 1)
    unit(2, 3)
    a_pair(6)
    a_near(7)
    give(5, 2)
    products(4, (3,))
    give(4, 3)
    give(5, 3)
    products(6, every, 0, 6)
    a_pair(7)
    a_done(6)
    products(6, every, 6, 8)
    products(7, every, 0, 6)
    gather(0)
    finish(6, 0)
    a_done(7)
    products(7, every, 6, 8)
    finish(7, 0)
    gather(1)
    finish(6, 1)
    finish(7, 1)
    gather(2)
    finish(6, 2)
    finish(7, 2)
    last_waits()
    gather(3)
    finish(6, 3)
    finish(7, 3)

    def flip_out(j, carry):
        for half in range(2):
            out_ref[half, j] = jnp.concatenate([own[half, h, j] for h in range(PARTS)], axis=0).T
        return carry

    def row_exchange():
        for d in range(1, 8):
            send(t1.at[r], t1.at[r], t1_sem, (d - 1,), row_peers[d - 1])
        for d in range(1, 8):
            arrive(t1.at[(r + 8 - d) % 8], t1_sem, (d - 1,))
        t2[f] = jnp.sum(t1[...], axis=0)

    def layer_exchange():
        for d in range(1, 4):
            send(t2.at[f], t2.at[f], t2_sem, (d - 1,), fib_peers[d - 1])
        lax.fori_loop(0, 16, flip_out, 0)
        for d in range(1, 4):
            arrive(t2.at[(f + 4 - d) % 4], t2_sem, (d - 1,))
        gain_ref[...] = total_rows / (jnp.sum(t2[...], axis=0) + epsilon)

    row_exchange()
    layer_exchange()
    last_waits()


def on_device(a_tiles, a_cols, a_count, b_tiles, b_cols):
    block_rows = b_tiles.shape[0]
    total_rows = 8 * lax.axis_size("row") * TILE
    dma = pltpu.SemaphoreType.DMA
    any_ = pl.BlockSpec(memory_space=pl.ANY)
    squares, gains = pl.pallas_call(
        functools.partial(kernel, total_rows, lax.axis_size("fiber")),
        out_shape=(pltpu.VMEM((2, 16, TILE, TILE), F32), pltpu.VMEM((16, TILE), F32)),
        in_specs=[any_] * 5,
        out_specs=(pl.BlockSpec(memory_space=pltpu.VMEM),) * 2,
        scratch_shapes=[
            pltpu.VMEM((8, 8, ASLOTS, TILE, TILE), jnp.bfloat16),
            *[pltpu.VMEM((512, WIDE, TILE), jnp.bfloat16)] * PARTS,
            pltpu.VMEM((64, TILE, TILE), jnp.bfloat16),
            pltpu.VMEM((8, 8, ASLOTS), jnp.int32),
            pltpu.VMEM((8, 1, 8), jnp.int32),
            pltpu.VMEM((8, 1, 64), jnp.int32),
            pltpu.VMEM((8, 8, TILE), jnp.int32),
            pltpu.SMEM((8, 8, TILE), jnp.int32),
            pltpu.VMEM((3 * PARTS, 1 + 8 * ASLOTS, WIDE, TILE), F32),
            pltpu.VMEM((6 * PARTS, 16, WIDE, TILE), jnp.int16),
            pltpu.VMEM((6 * PARTS, 4, TILE), F32),
            pltpu.VMEM((6 * PARTS, 16, WIDE, TILE), jnp.int16),
            pltpu.VMEM((6 * PARTS, 4, TILE), F32),
            pltpu.VMEM((2, PARTS, 16, WIDE, TILE), F32),
            pltpu.VMEM((8, 16, TILE), F32),
            pltpu.VMEM((4, 16, TILE), F32),
            dma((5 + PIECES,)),
            dma((2, 7)),
            dma((2, 7)),
            dma((2, 7)),
            dma((2, 8, 3)),
            dma((2, 8, 2)),
            dma((2, 8, 4)),
            dma((2, PARTS, PIECES, 3)),
            dma((2, PARTS, PIECES, 3)),
            dma((2, PARTS, PIECES)),
            dma((2, 6 * PARTS)),
            dma((2, 6 * PARTS)),
            dma((2, 7)),
            dma((2, 3)),
        ],
        compiler_params=pltpu.CompilerParams(collective_id=0, has_side_effects=True, vmem_limit_bytes=56 * 1024 * 1024),
    )(a_cols, a_count.reshape(1, 8), b_cols.reshape(1, block_rows), a_tiles, b_tiles.reshape(block_rows, TILE, TILE))
    return squares * gains[None, :, None, :]


def solution(mesh):
    placed = (
        P("row", ("col", "fiber"), None, None),
        P("row", ("col", "fiber")),
        P("row", ("col", "fiber")),
        P(("row", "fiber"), "col", None, None),
        P(("row", "fiber"), "col"),
    )
    return jax.shard_map(
        on_device,
        mesh=mesh,
        in_specs=placed,
        out_specs=P(("row", "fiber"), "col", None, None),
        check_vma=False,
    )
```

time: 150 us -> 141 us (0.940)
  Pallas kernels: 146 us -> 139 us
  other arithmetic: 3.67 us -> 1.57 us
    pallas_call x1, Pallas kernels: 146 us -> 139 us  [on_device(): pl.pallas_call(functools.partial(kernel, total_rows, lax.axis_size('fiber...]
where the time goes in v3:
time: 141 us
  Pallas kernels  139 us (99%)
  other arithmetic  1.57 us (1%)
    pallas_call x1, Pallas kernels, on_device(): pl.pallas_call(functools.partial(kernel, total_rows, lax.axis_size('fiber...  139 us

profile of v3, /device:TPU:1, one launch (start us, length us, event | category | flops | bytes accessed | tf_op | source)
XLA Modules:
  0.0 140.9 jit_solution(867256756353430658)
XLA Ops:
  0.0 139.3 %shard_map.55 = (f32[2,16,128,128]{3,2,1,0:T(8,128)S(1)}, f32[16,128]{1,0:T(8,128)S(1)}) custom-call(s32[8,6]{1,0:T(8,128)} %cols_ref.1, s32[1,8]{1,0:T(1,128)} %bitcast.4, s32[1,64]{1,0:T(1,128)} %bitcast.5, bf16[8,6,128,128]{3,2,1,0:T(8,128)(2,1)} %a_ref.1, bf16[64,128,128]{2,1,0:T(8,128)(2,1)} %bitcast.3), custom_call_target="tpu_custom_call" | custom-call | tf_op jit(solution)/shard_map/pallas_call | solution.py:483
  139.3 1.6 %broadcast_multiply_fusion = f32[2,16,128,128]{3,2,1,0:T(8,128)} fusion(f32[2,16,128,128]{3,2,1,0:T(8,128)S(1)} %get-tuple-element.7, f32[16,128]{1,0:T(8,128)S(1)} %get-tuple-element.8), kind=kLoop, calls=%fused_computation | loop fusion | flops 524288 | bytes 4202496 | tf_op jit(solution)/shard_map/mul | solution.py:522

commit v4 on v3

--- a/solution.py
+++ b/solution.py
@@ -20,8 +20,8 @@
 TOP = 32767.0
 
 
-def kernel(total_rows, fibers, cols_ref, count_ref, target_ref, a_ref, b_ref, out_ref, gain_ref, pa, pb0, pb1, pb2, pb3, raw_b, ma, mn, mb, meta_v, meta_s, sums, cq_s, cs_s, cq_r, cs_r, own,
-           t1, t2, loc_sem, ma_sem, mn_sem, mb_sem, ao_sem, ap_sem, af_sem, bo_sem, bk_sem, bf_sem, cq_sem, cs_sem, t1_sem, t2_sem):
+def kernel(total_rows, fibers, cols_ref, count_ref, target_ref, a_ref, b_ref, result_ref, gain_ref, pa, pb0, pb1, pb2, pb3, raw_b, ma, mn, mb, meta_v, meta_s, sums, cq_s, cs_s, cq_r, cs_r, own, out_ref,
+           t1, t2, loc_sem, out_sem, m_sem, ao_sem, ap_sem, af_sem, bn_sem, bf_sem, kp_sem, far_sem, sum_sem, t_sem):
     r, c, f = lax.axis_index("row"), lax.axis_index("col"), lax.axis_index("fiber")
     x, k = r // 2, r % 2
     zl, y = c // 4, c % 4
@@ -70,19 +70,23 @@
         sums[q, 0] = jnp.zeros((WIDE, TILE), F32)
 
     sum_set = (0, 0, 0, 0, 1, 2, 0, 1)
-    started = []
-
-    def send(src, dst, sem, at, device):
-        copy = pltpu.make_async_remote_copy(
-            src_ref=src, dst_ref=dst, send_sem=sem.at[(0,) + at], recv_sem=sem.at[(1,) + at], device_id=device, device_id_type=MESH
-        )
-        copy.start()
-        started.append(copy)
-
-    def arrive(dst, sem, at):
+
+    def send(src, dst, out, into, device):
         pltpu.make_async_remote_copy(
-            src_ref=dst, dst_ref=dst, send_sem=sem.at[(0,) + at], recv_sem=sem.at[(1,) + at], device_id=KP, device_id_type=MESH
+            src_ref=src, dst_ref=dst, send_sem=out_sem.at[out], recv_sem=into, device_id=device, device_id_type=MESH
+        ).start()
+
+    def arrive(dst, into):
+        pltpu.make_async_remote_copy(
+            src_ref=dst, dst_ref=dst, send_sem=out_sem.at[0], recv_sem=into, device_id=KP, device_id_type=MESH
         ).wait_recv()
+
+    def left(src, out):
+        pltpu.make_async_remote_copy(
+            src_ref=src, dst_ref=src, send_sem=out_sem.at[out], recv_sem=m_sem.at[0], device_id=KP, device_id_type=MESH
+        ).wait_send()
+
+    AO, AP, AF, CQ, CS, MA, MN, MB, T1, T2, BO, BK, BF = 0, 1, 2, 3, 4, 5, 6, 7, 8, 9, 10, 14, 18
 
     def flip_b(q):
         def one_tile(n, carry):
@@ -99,9 +103,9 @@
 
     def b_own(h, q):
         part = b_at(h, r, q)
-        send(part, part, bo_sem, (h, q, 1), XP)
-        send(part, part, bo_sem, (h, q, 2), XM)
-        send(part, part, bo_sem, (h, q, 0), KP)
+        send(part, part, BO + h, bn_sem.at[h, q, 0], XP)
+        send(part, part, BO + h, bn_sem.at[h, q, 1], XM)
+        send(part, part, BO + h, kp_sem.at[h], KP)
 
     def b_all(h):
         for q in range(PIECES):
@@ -109,28 +113,24 @@
 
     def b_near(h, q):
         part = b_at(h, rid(-1, k), q)
-        arrive(part, bo_sem, (h, q, 1))
+        arrive(part, bn_sem.at[h, q, 0])
         if q < PIECES // 2:
-            send(part, part, bf_sem, (h, q), XP)
-        send(part, part, bk_sem, (h, q, 0), KP)
+            send(part, part, BF + h, bf_sem.at[h, q], XP)
+        send(part, part, BK + h, kp_sem.at[h], KP)
         part = b_at(h, rid(1, k), q)
-        arrive(part, bo_sem, (h, q, 2))
+        arrive(part, bn_sem.at[h, q, 1])
         if q >= PIECES // 2:
-            send(part, part, bf_sem, (h, q), XM)
-        send(part, part, bk_sem, (h, q, 1), KP)
+            send(part, part, BF + h, bf_sem.at[h, q], XM)
+        send(part, part, BK + h, kp_sem.at[h], KP)
 
     def b_far(h, q):
         for at in (q, q + PIECES // 2):
             part = b_at(h, rid(2, k), at)
-            arrive(part, bf_sem, (h, at))
-            send(part, part, bk_sem, (h, at, 2), KP)
+            arrive(part, bf_sem.at[h, at])
+            send(part, part, BK + h, kp_sem.at[h], KP)
 
     def b_done(h):
-        for q in range(PIECES):
-            arrive(b_at(h, rid(0, 1 - k), q), bo_sem, (h, q, 0))
-            arrive(b_at(h, rid(-1, 1 - k), q), bk_sem, (h, q, 0))
-            arrive(b_at(h, rid(1, 1 - k), q), bk_sem, (h, q, 1))
-            arrive(b_at(h, rid(2, 1 - k), q), bk_sem, (h, q, 2))
+        arrive(pb[h].at[pl.ds(0, 256)], kp_sem.at[h])
 
     rows = [far * 2, far * 2 + 1, plus * 2 + 1, minus * 2, plus * 2, minus * 2 + 1, f * 2, f * 2 + 1]
     pair_rows = [far * 2, far * 2 + 1, minus * 2 + 1, plus * 2, minus * 2, plus * 2 + 1, f * 2, f * 2 + 1]
@@ -139,48 +139,44 @@
         for way, device in enumerate((ZP, YP, YM)):
             row = rows[n] if way else pair_rows[n]
             if way in ways:
-                send(a_ref.at[row], pa.at[row, c], ao_sem, (n, way), device)
-
-    def a_half(n, block, half, way, device):
+                send(a_ref.at[row], pa.at[row, c], AO, ao_sem.at[n, way], device)
+
+    def a_half(n, block, half, device):
         part = pa.at[rows[n], block, pl.ds(half * 3, 3)]
-        send(part, part, af_sem, (n, way), device)
+        send(part, part, AF, af_sem.at[n], device)
 
     def a_near(n):
         row = rows[n]
         block = cid(0, 1 - zl)
-        arrive(pa.at[row, block], ao_sem, (n, 0))
+        arrive(pa.at[row, block], ao_sem.at[n, 0])
         for way, device in enumerate((YP, YM)):
-            send(pa.at[row, block], pa.at[row, block], ap_sem, (n, way), device)
-        arrive(pa.at[row, cid(-1, zl)], ao_sem, (n, 1))
-        a_half(n, cid(-1, zl), 0, 0, YP)
-        arrive(pa.at[row, cid(1, zl)], ao_sem, (n, 2))
-        a_half(n, cid(1, zl), 1, 1, YM)
+            send(pa.at[row, block], pa.at[row, block], AP, ap_sem.at[n, way], device)
+        arrive(pa.at[row, cid(-1, zl)], ao_sem.at[n, 1])
+        a_half(n, cid(-1, zl), 0, YP)
+        arrive(pa.at[row, cid(1, zl)], ao_sem.at[n, 2])
+        a_half(n, cid(1, zl), 1, YM)
         if n < 2:
             for later in range(3 + n * 3, min(6 + n * 3, 8)):
                 a_own(later, (0,))
 
     def a_pair(n):
         row = rows[n]
-        arrive(pa.at[row, cid(-1, 1 - zl)], ap_sem, (n, 0))
-        a_half(n, cid(-1, 1 - zl), 0, 2, YP)
-        arrive(pa.at[row, cid(1, 1 - zl)], ap_sem, (n, 1))
-        a_half(n, cid(1, 1 - zl), 1, 3, YM)
+        arrive(pa.at[row, cid(-1, 1 - zl)], ap_sem.at[n, 0])
+        a_half(n, cid(-1, 1 - zl), 0, YP)
+        arrive(pa.at[row, cid(1, 1 - zl)], ap_sem.at[n, 1])
+        a_half(n, cid(1, 1 - zl), 1, YM)
         if n + 2 < 8:
             a_own(n + 2, (1, 2))
 
     def a_done(n):
-        row = rows[n]
-        for way, (zz, half) in enumerate(((zl, 0), (zl, 1), (1 - zl, 0), (1 - zl, 1))):
-            arrive(pa.at[row, cid(2, zz), pl.ds(half * 3, 3)], af_sem, (n, way))
+        arrive(pa.at[rows[n], pl.ds(0, 2)], af_sem.at[n])
 
     def block_of(o):
         return ((zl + o) % 2) * 4 + (y + o // 2 + 3) % 4
 
     def index_tables():
-        for d in range(1, 8):
-            arrive(ma.at[(c + 8 - d) % 8], ma_sem, (d - 1,))
-            arrive(mn.at[(c + 8 - d) % 8], mn_sem, (d - 1,))
-            arrive(mb.at[(r + 8 - d) % 8], mb_sem, (d - 1,))
+        for n, ref in enumerate((ma, mn, mb)):
+            arrive(ref.at[pl.ds(0, 7)], m_sem.at[n])
         lane = lax.broadcasted_iota(jnp.int32, (64, TILE), 1)
         slot = lax.broadcasted_iota(jnp.int32, (64, TILE), 0)
         kept = slot - (SLOTS8 - ASLOTS) * (slot // SLOTS8) + 1
@@ -238,7 +234,7 @@
                     sums[into + h, 1 + o * ASLOTS + e] = product[n_h * WIDE : (n_h + 1) * WIDE] + sums[into + h, prev]
             return carry
 
-        lax.fori_loop(first, stop, one_block, 0)
+        lax.fori_loop(first, stop, one_block, 0, unroll=4 if stop - first == 8 else 2)
 
     wide_lane = lax.broadcasted_iota(jnp.int32, (WIDE, TILE), 1)
     wide_slot = lax.broadcasted_iota(jnp.int32, (WIDE, TILE), 0)
@@ -254,14 +250,15 @@
 
     def emit(n, h, at, device, add=None):
         row = rows[n]
-        at = at * PARTS + h
+        slot = at
+        at = h * 6 + at
 
         def four_tiles(g, carry):
             scales = jnp.zeros((1, TILE), F32)
             for i in range(4):
                 value = sums[PARTS * sum_set[n] + h, meta_s[row, 2, g * 4 + i]]
                 if add is not None:
-                    value = value + decoded(add * PARTS + h, g, i)
+                    value = value + decoded(h * 6 + add, g, i)
                 top = jnp.max(jnp.abs(value), axis=1, keepdims=True)
                 gain = jnp.where(top > 1e-30, TOP / jnp.maximum(top, 1e-30), 0.0)
                 cq_s[at, g * 4 + i] = jnp.floor(value * gain + 0.5).astype(jnp.int32).astype(jnp.int16)
@@ -270,22 +267,22 @@
             return carry
 
         lax.fori_loop(0, 4, four_tiles, 0)
-        send(cs_s.at[at], cs_r.at[at], cs_sem, (at,), device)
-        send(cq_s.at[at], cq_r.at[at], cq_sem, (at,), device)
+        into = [far_sem.at[n, slot, h] if slot < 2 else sum_sem.at[n, h] for n in range(2)]
+        send(cs_s.at[at], cs_r.at[at], CS, into[0], device)
+        send(cq_s.at[at], cq_r.at[at], CQ, into[1], device)
 
     def c_arrive(at, h):
-        at = at * PARTS + h
-        arrive(cs_r.at[at], cs_sem, (at,))
-        arrive(cq_r.at[at], cq_sem, (at,))
+        arrive(cs_r.at[h * 6 + at], far_sem.at[0, at, h])
+        arrive(cq_r.at[h * 6 + at], far_sem.at[1, at, h])
 
     def gather(h):
-        for at in (3, 4, 2, 5):
-            c_arrive(at, h)
+        arrive(cs_r.at[pl.ds(h * 6 + 2, 4)], sum_sem.at[0, h])
+        arrive(cq_r.at[pl.ds(h * 6 + 2, 4)], sum_sem.at[1, h])
 
         def four_tiles(g, carry):
             for i in range(4):
                 for half in range(2):
-                    own[half, h, g * 4 + i] = decoded((2 + half) * PARTS + h, g, i) + decoded((4 + half) * PARTS + h, g, i)
+                    own[half, h, g * 4 + i] = decoded(h * 6 + 2 + half, g, i) + decoded(h * 6 + 4 + half, g, i)
             return carry
 
         lax.fori_loop(0, 4, four_tiles, 0)
@@ -330,9 +327,9 @@
         for n in (0, 1, -1):
             locals_[n].wait()
         for d in range(1, 8):
-            send(ma.at[c], ma.at[c], ma_sem, (d - 1,), col_peers[d - 1])
-            send(mn.at[c], mn.at[c], mn_sem, (d - 1,), col_peers[d - 1])
-            send(mb.at[r], mb.at[r], mb_sem, (d - 1,), row_peers[d - 1])
+            send(ma.at[c], ma.at[c], MA, m_sem.at[0], col_peers[d - 1])
+            send(mn.at[c], mn.at[c], MN, m_sem.at[1], col_peers[d - 1])
+            send(mb.at[r], mb.at[r], MB, m_sem.at[2], row_peers[d - 1])
 
     def start_b():
         flip_b(1)
@@ -345,21 +342,30 @@
         b_own(0, 3)
 
     def last_waits():
-        for copy in started:
-            copy.wait_send()
-        started.clear()
+        left(pa.at[pl.ds(0, 3)], AO)
+        left(pa.at[pl.ds(0, 2)], AP)
+        left(pa.at[pl.ds(0, 2)], AF)
+        left(cq_s, CQ)
+        left(cs_s, CS)
+        left(ma.at[pl.ds(0, 7)], MA)
+        left(mn.at[pl.ds(0, 7)], MN)
+        left(mb.at[pl.ds(0, 7)], MB)
+        for h in range(PARTS):
+            left(pb[h].at[pl.ds(0, 192)], BO + h)
+            left(pb[h].at[pl.ds(0, 192)], BK + h)
+            left(pb[h].at[pl.ds(0, 64)], BF + h)
 
     start()
     start_b()
     b_near(0, 0)
     a_near(0)
     b_near(0, 1)
+    index_tables()
     b_near(0, 2)
     b_near(0, 3)
     b_all(1)
     a_pair(0)
     a_near(1)
-    index_tables()
     b_far(0, 0)
     b_far(0, 1)
     b_done(0)
@@ -367,9 +373,9 @@
     unit(0, 0)
     b_near(1, 0)
     b_near(1, 1)
+    b_near(1, 2)
     a_pair(1)
     a_near(2)
-    b_near(1, 2)
     b_near(1, 3)
     b_all(2)
     a_done(1)
@@ -377,10 +383,10 @@
     b_far(1, 0)
     b_far(1, 1)
     b_done(1)
+    unit(0, 1)
+    b_near(2, 0)
     a_pair(2)
     a_near(3)
-    unit(0, 1)
-    b_near(2, 0)
     unit(1, 1)
     b_near(2, 1)
     b_near(2, 2)
@@ -399,48 +405,48 @@
     b_near(3, 1)
     a_done(3)
     unit(3, 0, 1)
+    b_near(3, 2)
+    b_near(3, 3)
     a_pair(4)
     a_near(5)
-    b_near(3, 2)
     unit(2, 2)
-    b_near(3, 3)
     unit(3, 2)
+    b_far(3, 0)
+    b_far(3, 1)
     a_done(4)
     products(4, (0, 1, 2))
-    give(4, 0)
-    b_far(3, 0)
-    b_far(3, 1)
     b_done(3)
     unit(1, 3)
     unit(0, 3)
+    give(4, 0)
+    give(4, 1)
     a_pair(5)
     a_near(6)
-    give(4, 1)
+    give(4, 2)
     unit(3, 3)
+    unit(2, 3)
+    products(4, (3,))
     a_done(5)
     products(5, every)
     give(5, 0)
-    give(4, 2)
     give(5, 1)
-    unit(2, 3)
+    give(5, 2)
+    give(4, 3)
     a_pair(6)
     a_near(7)
-    give(5, 2)
-    products(4, (3,))
-    give(4, 3)
+    products(6, every, 0, 6)
     give(5, 3)
-    products(6, every, 0, 6)
-    a_pair(7)
     a_done(6)
     products(6, every, 6, 8)
+    a_pair(7)
     products(7, every, 0, 6)
     gather(0)
     finish(6, 0)
+    gather(1)
+    finish(6, 1)
     a_done(7)
     products(7, every, 6, 8)
     finish(7, 0)
-    gather(1)
-    finish(6, 1)
     finish(7, 1)
     gather(2)
     finish(6, 2)
@@ -450,29 +456,36 @@
     finish(6, 3)
     finish(7, 3)
 
-    def flip_out(j, carry):
-        for half in range(2):
+    results = [pltpu.make_async_copy(out_ref.at[half], result_ref.at[half], loc_sem.at[5 + PIECES + half]) for half in range(2)]
+
+    def flip_out(half):
+        def one_tile(j, carry):
             out_ref[half, j] = jnp.concatenate([own[half, h, j] for h in range(PARTS)], axis=0).T
-        return carry
+            return carry
+
+        lax.fori_loop(0, 16, one_tile, 0)
+        results[half].start()
 
     def row_exchange():
         for d in range(1, 8):
-            send(t1.at[r], t1.at[r], t1_sem, (d - 1,), row_peers[d - 1])
-        for d in range(1, 8):
-            arrive(t1.at[(r + 8 - d) % 8], t1_sem, (d - 1,))
+            send(t1.at[r], t1.at[r], T1, t_sem.at[0], row_peers[d - 1])
+        flip_out(0)
+        arrive(t1.at[pl.ds(0, 7)], t_sem.at[0])
         t2[f] = jnp.sum(t1[...], axis=0)
 
     def layer_exchange():
         for d in range(1, 4):
-            send(t2.at[f], t2.at[f], t2_sem, (d - 1,), fib_peers[d - 1])
-        lax.fori_loop(0, 16, flip_out, 0)
-        for d in range(1, 4):
-            arrive(t2.at[(f + 4 - d) % 4], t2_sem, (d - 1,))
+            send(t2.at[f], t2.at[f], T2, t_sem.at[1], fib_peers[d - 1])
+        flip_out(1)
+        arrive(t2.at[pl.ds(0, 3)], t_sem.at[1])
         gain_ref[...] = total_rows / (jnp.sum(t2[...], axis=0) + epsilon)
+        for copy in results:
+            copy.wait()
 
     row_exchange()
     layer_exchange()
-    last_waits()
+    left(t1.at[pl.ds(0, 7)], T1)
+    left(t2.at[pl.ds(0, 3)], T2)
 
 
 def on_device(a_tiles, a_cols, a_count, b_tiles, b_cols):
@@ -484,7 +497,7 @@
         functools.partial(kernel, total_rows, lax.axis_size("fiber")),
         out_shape=(pltpu.VMEM((2, 16, TILE, TILE), F32), pltpu.VMEM((16, TILE), F32)),
         in_specs=[any_] * 5,
-        out_specs=(pl.BlockSpec(memory_space=pltpu.VMEM),) * 2,
+        out_specs=(any_, pl.BlockSpec(memory_space=pltpu.VMEM)),
         scratch_shapes=[
             pltpu.VMEM((8, 8, ASLOTS, TILE, TILE), jnp.bfloat16),
             *[pltpu.VMEM((512, WIDE, TILE), jnp.bfloat16)] * PARTS,
@@ -500,22 +513,21 @@
             pltpu.VMEM((6 * PARTS, 16, WIDE, TILE), jnp.int16),
             pltpu.VMEM((6 * PARTS, 4, TILE), F32),
             pltpu.VMEM((2, PARTS, 16, WIDE, TILE), F32),
+            pltpu.VMEM((2, 16, TILE, TILE), F32),
             pltpu.VMEM((8, 16, TILE), F32),
             pltpu.VMEM((4, 16, TILE), F32),
-            dma((5 + PIECES,)),
-            dma((2, 7)),
-            dma((2, 7)),
-            dma((2, 7)),
-            dma((2, 8, 3)),
-            dma((2, 8, 2)),
-            dma((2, 8, 4)),
-            dma((2, PARTS, PIECES, 3)),
-            dma((2, PARTS, PIECES, 3)),
-            dma((2, PARTS, PIECES)),
-            dma((2, 6 * PARTS)),
-            dma((2, 6 * PARTS)),
-            dma((2, 7)),
-            dma((2, 3)),
+            dma((7 + PIECES,)),
+            dma((22,)),
+            dma((3,)),
+            dma((8, 3)),
+            dma((8, 2)),
+            dma((8,)),
+            dma((PARTS, PIECES, 2)),
+            dma((PARTS, PIECES)),
+            dma((PARTS,)),
+            dma((2, 2, PARTS)),
+            dma((2, PARTS)),
+            dma((2,)),
         ],
         compiler_params=pltpu.CompilerParams(collective_id=0, has_side_effects=True, vmem_limit_bytes=56 * 1024 * 1024),
     )(a_cols, a_count.reshape(1, 8), b_cols.reshape(1, block_rows), a_tiles, b_tiles.reshape(block_rows, TILE, TILE))

time: 141 us -> 136 us (0.965)
  Pallas kernels: 139 us -> 134 us
    pallas_call x1, Pallas kernels: 139 us -> 134 us  [on_device(): pl.pallas_call(functools.partial(kernel, total_rows, lax.axis_size('fiber...]
where the time goes in v4:
time: 136 us
  Pallas kernels  134 us (99%)
  other arithmetic  1.57 us (1%)
    pallas_call x1, Pallas kernels, on_device(): pl.pallas_call(functools.partial(kernel, total_rows, lax.axis_size('fiber...  134 us

profile of v4, /device:TPU:1, one launch (start us, length us, event | category | flops | bytes accessed | tf_op | source)
XLA Modules:
  0.0 136.1 jit_solution(4180568877419566599)
XLA Ops:
  0.0 134.5 %shard_map.55 = (f32[2,16,128,128]{3,2,1,0:T(8,128)S(1)}, f32[16,128]{1,0:T(8,128)S(1)}) custom-call(s32[8,6]{1,0:T(8,128)} %cols_ref.1, s32[1,8]{1,0:T(1,128)} %bitcast.4, s32[1,64]{1,0:T(1,128)} %bitcast.5, bf16[8,6,128,128]{3,2,1,0:T(8,128)(2,1)} %a_ref.1, bf16[64,128,128]{2,1,0:T(8,128)(2,1)} %bitcast.3), custom_call_target="tpu_custom_call" | custom-call | tf_op jit(solution)/shard_map/pallas_call | solution.py:496
  134.5 1.6 %broadcast_multiply_fusion = f32[2,16,128,128]{3,2,1,0:T(8,128)} fusion(f32[2,16,128,128]{3,2,1,0:T(8,128)S(1)} %get-tuple-element.7, f32[16,128]{1,0:T(8,128)S(1)} %get-tuple-element.8), kind=kLoop, calls=%fused_computation | loop fusion | flops 524288 | bytes 4202496 | tf_op jit(solution)/shard_map/mul | solution.py:534

commit v5 on v4

--- a/solution.py
+++ b/solution.py
@@ -103,8 +103,8 @@
 
     def b_own(h, q):
         part = b_at(h, r, q)
-        send(part, part, BO + h, bn_sem.at[h, q, 0], XP)
-        send(part, part, BO + h, bn_sem.at[h, q, 1], XM)
+        send(part, part, BO + h, bn_sem.at[h, q], XP)
+        send(part, part, BO + h, bn_sem.at[h, q], XM)
         send(part, part, BO + h, kp_sem.at[h], KP)
 
     def b_all(h):
@@ -112,21 +112,19 @@
             b_own(h, q)
 
     def b_near(h, q):
-        part = b_at(h, rid(-1, k), q)
-        arrive(part, bn_sem.at[h, q, 0])
+        arrive(pb[h].at[pl.ds(0, 2 * piece)], bn_sem.at[h, q])
+        up, down = b_at(h, rid(-1, k), q), b_at(h, rid(1, k), q)
         if q < PIECES // 2:
-            send(part, part, BF + h, bf_sem.at[h, q], XP)
-        send(part, part, BK + h, kp_sem.at[h], KP)
-        part = b_at(h, rid(1, k), q)
-        arrive(part, bn_sem.at[h, q, 1])
-        if q >= PIECES // 2:
-            send(part, part, BF + h, bf_sem.at[h, q], XM)
-        send(part, part, BK + h, kp_sem.at[h], KP)
+            send(up, up, BF + h, bf_sem.at[h, q], XP)
+        else:
+            send(down, down, BF + h, bf_sem.at[h, q - PIECES // 2], XM)
+        send(up, up, BK + h, kp_sem.at[h], KP)
+        send(down, down, BK + h, kp_sem.at[h], KP)
 
     def b_far(h, q):
+        arrive(pb[h].at[pl.ds(0, 2 * piece)], bf_sem.at[h, q])
         for at in (q, q + PIECES // 2):
             part = b_at(h, rid(2, k), at)
-            arrive(part, bf_sem.at[h, at])
             send(part, part, BK + h, kp_sem.at[h], KP)
 
     def b_done(h):
@@ -139,7 +137,7 @@
         for way, device in enumerate((ZP, YP, YM)):
             row = rows[n] if way else pair_rows[n]
             if way in ways:
-                send(a_ref.at[row], pa.at[row, c], AO, ao_sem.at[n, way], device)
+                send(a_ref.at[row], pa.at[row, c], AO, ao_sem.at[n, min(way, 1)], device)
 
     def a_half(n, block, half, device):
         part = pa.at[rows[n], block, pl.ds(half * 3, 3)]
@@ -149,11 +147,10 @@
         row = rows[n]
         block = cid(0, 1 - zl)
         arrive(pa.at[row, block], ao_sem.at[n, 0])
-        for way, device in enumerate((YP, YM)):
-            send(pa.at[row, block], pa.at[row, block], AP, ap_sem.at[n, way], device)
-        arrive(pa.at[row, cid(-1, zl)], ao_sem.at[n, 1])
+        for device in (YP, YM):
+            send(pa.at[row, block], pa.at[row, block], AP, ap_sem.at[n], device)
+        arrive(pa.at[row, pl.ds(0, 2)], ao_sem.at[n, 1])
         a_half(n, cid(-1, zl), 0, YP)
-        arrive(pa.at[row, cid(1, zl)], ao_sem.at[n, 2])
         a_half(n, cid(1, zl), 1, YM)
         if n < 2:
             for later in range(3 + n * 3, min(6 + n * 3, 8)):
@@ -161,9 +158,8 @@
 
     def a_pair(n):
         row = rows[n]
-        arrive(pa.at[row, cid(-1, 1 - zl)], ap_sem.at[n, 0])
+        arrive(pa.at[row, pl.ds(0, 2)], ap_sem.at[n])
         a_half(n, cid(-1, 1 - zl), 0, YP)
-        arrive(pa.at[row, cid(1, 1 - zl)], ap_sem.at[n, 1])
         a_half(n, cid(1, 1 - zl), 1, YM)
         if n + 2 < 8:
             a_own(n + 2, (1, 2))
@@ -304,10 +300,33 @@
 
         lax.fori_loop(0, 4, four_tiles, 0)
 
+    def finish_last(h):
+        arrive(cs_r.at[pl.ds(h * 6 + 2, 4)], sum_sem.at[0, h])
+        arrive(cq_r.at[pl.ds(h * 6 + 2, 4)], sum_sem.at[1, h])
+
+        def four_tiles(g, carry):
+            for i in range(4):
+                j = g * 4 + i
+                total = jnp.zeros((WIDE, TILE), F32)
+                for half in range(2):
+                    value = decoded(h * 6 + 2 + half, g, i) + decoded(h * 6 + 4 + half, g, i)
+                    value = value + sums[PARTS * sum_set[6 + half] + h, meta_s[rows[6 + half], 2, j]]
+                    value = value * value
+                    own[half, h, j] = value
+                    total = total + value
+                total = to_lanes(jnp.sum(total, axis=1, keepdims=True), h)
+                t1[r, pl.ds(j, 1), :] = t1[r, pl.ds(j, 1), :] + total
+            return carry
+
+        lax.fori_loop(0, 4, four_tiles, 0)
+
     slots = ((0, FP, None), (1, FM, None), (3, FP, None), (4, FM, None), (2, FP, 0), (5, FM, 1))
 
     def give(n, h):
         at, device, add = slots[n]
+        if h == PARTS - 1:
+            device = FP if n == 1 else device
+            add = {2: 1, 5: None}.get(n, add)
         if add is not None:
             c_arrive(add, h)
         emit(n, h, at, device, add)
@@ -406,36 +425,36 @@
     a_done(3)
     unit(3, 0, 1)
     b_near(3, 2)
+    unit(2, 2)
     b_near(3, 3)
+    unit(3, 2)
     a_pair(4)
     a_near(5)
-    unit(2, 2)
-    unit(3, 2)
     b_far(3, 0)
     b_far(3, 1)
     a_done(4)
     products(4, (0, 1, 2))
+    give(4, 0)
     b_done(3)
     unit(1, 3)
     unit(0, 3)
-    give(4, 0)
     give(4, 1)
     a_pair(5)
     a_near(6)
     give(4, 2)
     unit(3, 3)
-    unit(2, 3)
     products(4, (3,))
     a_done(5)
     products(5, every)
     give(5, 0)
     give(5, 1)
     give(5, 2)
+    give(5, 3)
+    unit(2, 3)
     give(4, 3)
     a_pair(6)
     a_near(7)
     products(6, every, 0, 6)
-    give(5, 3)
     a_done(6)
     products(6, every, 6, 8)
     a_pair(7)
@@ -452,9 +471,7 @@
     finish(6, 2)
     finish(7, 2)
     last_waits()
-    gather(3)
-    finish(6, 3)
-    finish(7, 3)
+    finish_last(3)
 
     results = [pltpu.make_async_copy(out_ref.at[half], result_ref.at[half], loc_sem.at[5 + PIECES + half]) for half in range(2)]
 
@@ -519,11 +536,11 @@
             dma((7 + PIECES,)),
             dma((22,)),
             dma((3,)),
-            dma((8, 3)),
             dma((8, 2)),
             dma((8,)),
-            dma((PARTS, PIECES, 2)),
+            dma((8,)),
             dma((PARTS, PIECES)),
+            dma((PARTS, PIECES // 2)),
             dma((PARTS,)),
             dma((2, 2, PARTS)),
             dma((2, PARTS)),

time: 136 us -> 135 us (level)
  no operation moved by 1% of the time
where the time goes in v5:
time: 135 us
  Pallas kernels  134 us (99%)
  other arithmetic  1.57 us (1%)
    pallas_call x1, Pallas kernels, on_device(): pl.pallas_call(functools.partial(kernel, total_rows, lax.axis_size('fiber...  134 us

profile of v5, /device:TPU:1, one launch (start us, length us, event | category | flops | bytes accessed | tf_op | source)
XLA Modules:
  0.0 135.4 jit_solution(3382483545944250842)
XLA Ops:
  0.0 133.8 %shard_map.55 = (f32[2,16,128,128]{3,2,1,0:T(8,128)S(1)}, f32[16,128]{1,0:T(8,128)S(1)}) custom-call(s32[8,6]{1,0:T(8,128)} %cols_ref.1, s32[1,8]{1,0:T(1,128)} %bitcast.4, s32[1,64]{1,0:T(1,128)} %bitcast.5, bf16[8,6,128,128]{3,2,1,0:T(8,128)(2,1)} %a_ref.1, bf16[64,128,128]{2,1,0:T(8,128)(2,1)} %bitcast.3), custom_call_target="tpu_custom_call" | custom-call | tf_op jit(solution)/shard_map/pallas_call | solution.py:513
  133.8 1.6 %broadcast_multiply_fusion = f32[2,16,128,128]{3,2,1,0:T(8,128)} fusion(f32[2,16,128,128]{3,2,1,0:T(8,128)S(1)} %get-tuple-element.7, f32[16,128]{1,0:T(8,128)S(1)} %get-tuple-element.8), kind=kLoop, calls=%fused_computation | loop fusion | flops 524288 | bytes 4202496 | tf_op jit(solution)/shard_map/mul | solution.py:551
